TPU v7x, 128 devices: a whole 4x4x4 slice. The times are simulated.
128 devices in a mesh: ctx: 32 (over y, z, x_lo), head: 4 (over x_hi, core).
Axes of the slice: x: 4 (x_hi: 2, x_lo: 2; x = x_hi * 2 + x_lo), y: 4, z: 4, core: 2. Of those that a mesh axis runs over, the one named last changes fastest.
Arguments:
- tokens: bfloat16 [16384, 1024], P('ctx'), may hold values from -24 to 24
- w_query: bfloat16 [1024, 1024], P(None, 'head'), may hold values from -0.1875 to 0.1875
- w_key: bfloat16 [1024, 1024], P(None, 'head'), may hold values from -0.1875 to 0.1875
- w_value: bfloat16 [1024, 1024], P(None, 'head'), may hold values from -0.1875 to 0.1875
- w_out: bfloat16 [1024, 1024], P('head'), may hold values from -0.1875 to 0.1875
- block_mask: int32 [128, 128], replicated, may hold values from 0 to 1, as said below
- block_order: int32 [128], replicated, may hold values from 0 to 127, each once
Outputs:
- mixed: bfloat16 [16384, 1024], P('ctx', 'head')
Inputs may be any that keep to these rules, and one draw needn't show every extreme that they name: `block_mask`: entries are 0 or 1 and every diagonal entry is 1. `block_order`: each initial block index appears once.
All inputs are finite; a program needn't handle non-finite values.
Results may differ from a plain program's by a relative error of at most 0.013.
Values may be sent and summed in bfloat16 or wider, within the bound.
A program may use at most 256 MiB of HBM per device.

v0:
```python
import jax
import jax.numpy as jnp
from jax import lax
from jax.sharding import PartitionSpec as P

HEAD_DIM = 64
BLOCK = 128


def from_behind(value, axis, steps):
    count = lax.axis_size(axis)
    pairs = [(source, (source + steps) % count) for source in range(count)]
    return lax.ppermute(value, axis, pairs)


def body(tokens, w_query, w_key, w_value, w_out, block_mask, block_order):
    tok_rows = tokens.shape[0]
    features = w_query.shape[1]
    heads_here = features // HEAD_DIM
    query_proj = jnp.dot(tokens, w_query, preferred_element_type=jnp.float32).astype(jnp.bfloat16)
    key_proj = jnp.dot(tokens, w_key, preferred_element_type=jnp.float32).astype(jnp.bfloat16)
    value_proj = jnp.dot(tokens, w_value, preferred_element_type=jnp.float32).astype(jnp.bfloat16)
    query_heads = query_proj.reshape(tok_rows, heads_here, HEAD_DIM)
    loop_size = lax.axis_size("ctx")
    position = lax.axis_index("ctx")
    blocks_here = tok_rows // BLOCK
    own_order = lax.dynamic_slice_in_dim(block_order, position * blocks_here, blocks_here)
    mask_rows = jnp.take(block_mask, own_order, axis=0)
    scale = HEAD_DIM ** (-0.5)

    def key_mask(first_row, count):
        key_blocks = (first_row + jnp.arange(count, dtype=jnp.int32)) // BLOCK
        key_orig = jnp.take(block_order, key_blocks)
        block_cols = jnp.take(mask_rows, key_orig, axis=1)
        return jnp.repeat(block_cols, BLOCK, axis=0) > 0

    def attend(running, key_piece, value_piece, allowed):
        row_max, row_sum, weighted = running
        count = key_piece.shape[0]
        key_heads = key_piece.reshape(count, heads_here, HEAD_DIM)
        value_heads = value_piece.reshape(count, heads_here, HEAD_DIM)
        scores = (
            jnp.einsum("qhd,khd->hqk", query_heads, key_heads, preferred_element_type=jnp.float32)
            * scale
        )
        tile_max = jnp.max(jnp.where(allowed[None], scores, -1e30), axis=2)
        new_max = jnp.maximum(row_max, tile_max)
        probs = jnp.where(allowed[None], jnp.exp(scores - new_max[:, :, None]), 0.0)
        factor = jnp.exp(row_max - new_max)
        row_sum = row_sum * factor + jnp.sum(probs, axis=2)
        partial_value = jnp.einsum(
            "hqk,khd->qhd",
            probs.astype(jnp.bfloat16),
            value_heads,
            preferred_element_type=jnp.float32,
        )
        weighted = weighted * jnp.transpose(factor)[:, :, None] + partial_value
        return (new_max, row_sum, weighted)

    def visit(running, key_piece, value_piece, first_row):
        allowed = key_mask(first_row, key_piece.shape[0])
        return attend(running, key_piece, value_piece, allowed)

    running = (
        jnp.full((heads_here, tok_rows), -1e30, jnp.float32),
        jnp.zeros((heads_here, tok_rows), jnp.float32),
        jnp.zeros((tok_rows, heads_here, HEAD_DIM), jnp.float32),
    )
    kv_pair = jnp.stack([key_proj, value_proj])
    running = visit(running, key_proj, value_proj, position * tok_rows)

    def turn_once(turn_index, loop_state):
        current, moving = loop_state
        moving = from_behind(moving, "ctx", 1)
        source = (position - turn_index) % loop_size
        return (visit(current, moving[0], moving[1], source * tok_rows), moving)

    running, kv_pair = lax.fori_loop(1, loop_size, turn_once, (running, kv_pair))
    row_max, row_sum, weighted = running
    attended = (
        (weighted / jnp.transpose(row_sum)[:, :, None])
        .astype(jnp.bfloat16)
        .reshape(tok_rows, features)
    )
    partial_out = jnp.dot(attended, w_out, preferred_element_type=jnp.float32)
    return lax.psum_scatter(
        partial_out.astype(jnp.bfloat16), "head", scatter_dimension=1, tiled=True
    )


def solution(mesh):
    placed = (
        P("ctx", None),
        P(None, "head"),
        P(None, "head"),
        P(None, "head"),
        P("head", None),
        P(),
        P(),
    )
    return jax.shard_map(
        body, mesh=mesh, in_specs=placed, out_specs=P("ctx", "head"), check_vma=False
    )
```

profile of v0, /device:TPU:1, one launch (start us, length us, event | category | flops | bytes accessed | tf_op | source)
XLA Modules:
  0.0 652.1 jit_solution(3261369388845336822)
XLA Ops:
  9.0 3.4 gather_fusion.3
  21.8 562.4 %while.21 = (s32[]{:T(128)}, f32[4,512]{1,0:T(4,128)S(1)}, f32[4,512]{1,0:T(4,128)S(1)}, f32[512,4,64]{0,2,1:T(8,128)S(1)}, bf16[2,512,256]{1,2,0:T(8,128)(2,1)}...) while((s32[]{:T(128)}, f32[4,512]{1,0:T(4,128)S(1)}, ...), condition=%wide.region_5.8_spmd, body=%wide.region_2.7_spmd.sunk | while | flops 280268800 | bytes 20372792 | solution.py:78
  23.8 3.3 gather_fusion
  30.2 11.4 %collective-permute-done = bf16[2,512,256]{1,2,0:T(8,128)(2,1)S(1)} collective-permute-done((bf16[2,512,256]{1,2,0:T(8,128)(2,1)}, bf16[2,512,256]{1,2,0:T(8,128)(2,1)S(1)}, u32[]{:S(2)}, u32[]{:S(2)}) %collective-permute-start) | collective-permute-done | bytes 524320 | tf_op jit(solution)/shard_map/while/body/eval_jaxpr/ppermute | solution.py:13
  45.5 3.3 gather_fusion
  51.8 10.3 %collective-permute-done = bf16[2,512,256]{1,2,0:T(8,128)(2,1)S(1)} collective-permute-done((bf16[2,512,256]{1,2,0:T(8,128)(2,1)}, bf16[2,512,256]{1,2,0:T(8,128)(2,1)S(1)}, u32[]{:S(2)}, u32[]{:S(2)}) %collective-permute-start) | collective-permute-done | bytes 524320 | tf_op jit(solution)/shard_map/while/body/eval_jaxpr/ppermute | solution.py:13
  65.9 3.3 gather_fusion
  72.2 9.3 %collective-permute-done = bf16[2,512,256]{1,2,0:T(8,128)(2,1)S(1)} collective-permute-done((bf16[2,512,256]{1,2,0:T(8,128)(2,1)}, bf16[2,512,256]{1,2,0:T(8,128)(2,1)S(1)}, u32[]{:S(2)}, u32[]{:S(2)}) %collective-permute-start) | collective-permute-done | bytes 524320 | tf_op jit(solution)/shard_map/while/body/eval_jaxpr/ppermute | solution.py:13
  85.5 3.3 gather_fusion
  91.8 8.4 %collective-permute-done = bf16[2,512,256]{1,2,0:T(8,128)(2,1)S(1)} collective-permute-done((bf16[2,512,256]{1,2,0:T(8,128)(2,1)}, bf16[2,512,256]{1,2,0:T(8,128)(2,1)S(1)}, u32[]{:S(2)}, u32[]{:S(2)}) %collective-permute-start) | collective-permute-done | bytes 524320 | tf_op jit(solution)/shard_map/while/body/eval_jaxpr/ppermute | solution.py:13
  104.1 3.3 gather_fusion
  110.4 7.5 %collective-permute-done = bf16[2,512,256]{1,2,0:T(8,128)(2,1)S(1)} collective-permute-done((bf16[2,512,256]{1,2,0:T(8,128)(2,1)}, bf16[2,512,256]{1,2,0:T(8,128)(2,1)S(1)}, u32[]{:S(2)}, u32[]{:S(2)}) %collective-permute-start) | collective-permute-done | bytes 524320 | tf_op jit(solution)/shard_map/while/body/eval_jaxpr/ppermute | solution.py:13
  121.8 3.3 gather_fusion
  128.1 6.6 %collective-permute-done = bf16[2,512,256]{1,2,0:T(8,128)(2,1)S(1)} collective-permute-done((bf16[2,512,256]{1,2,0:T(8,128)(2,1)}, bf16[2,512,256]{1,2,0:T(8,128)(2,1)S(1)}, u32[]{:S(2)}, u32[]{:S(2)}) %collective-permute-start) | collective-permute-done | bytes 524320 | tf_op jit(solution)/shard_map/while/body/eval_jaxpr/ppermute | solution.py:13
  138.6 3.3 gather_fusion
  144.9 6.1 collective-permute-done
  154.8 3.3 gather_fusion
  161.2 6.1 collective-permute-done
  171.1 3.3 gather_fusion
  177.5 6.1 collective-permute-done
  187.4 3.3 gather_fusion
  193.8 6.1 collective-permute-done
  203.7 3.3 gather_fusion
  210.1 6.1 collective-permute-done
  220.0 3.3 gather_fusion
  226.4 6.3 collective-permute-done
  236.5 3.3 gather_fusion
  242.9 7.4 %collective-permute-done = bf16[2,512,256]{1,2,0:T(8,128)(2,1)S(1)} collective-permute-done((bf16[2,512,256]{1,2,0:T(8,128)(2,1)}, bf16[2,512,256]{1,2,0:T(8,128)(2,1)S(1)}, u32[]{:S(2)}, u32[]{:S(2)}) %collective-permute-start) | collective-permute-done | bytes 524320 | tf_op jit(solution)/shard_map/while/body/eval_jaxpr/ppermute | solution.py:13
  260.5 8.5 %collective-permute-done = bf16[2,512,256]{1,2,0:T(8,128)(2,1)S(1)} collective-permute-done((bf16[2,512,256]{1,2,0:T(8,128)(2,1)}, bf16[2,512,256]{1,2,0:T(8,128)(2,1)S(1)}, u32[]{:S(2)}, u32[]{:S(2)}) %collective-permute-start) | collective-permute-done | bytes 524320 | tf_op jit(solution)/shard_map/while/body/eval_jaxpr/ppermute | solution.py:13
  279.1 9.5 %collective-permute-done = bf16[2,512,256]{1,2,0:T(8,128)(2,1)S(1)} collective-permute-done((bf16[2,512,256]{1,2,0:T(8,128)(2,1)}, bf16[2,512,256]{1,2,0:T(8,128)(2,1)S(1)}, u32[]{:S(2)}, u32[]{:S(2)}) %collective-permute-start) | collective-permute-done | bytes 524320 | tf_op jit(solution)/shard_map/while/body/eval_jaxpr/ppermute | solution.py:13
  298.9 10.6 %collective-permute-done = bf16[2,512,256]{1,2,0:T(8,128)(2,1)S(1)} collective-permute-done((bf16[2,512,256]{1,2,0:T(8,128)(2,1)}, bf16[2,512,256]{1,2,0:T(8,128)(2,1)S(1)}, u32[]{:S(2)}, u32[]{:S(2)}) %collective-permute-start) | collective-permute-done | bytes 524320 | tf_op jit(solution)/shard_map/while/body/eval_jaxpr/ppermute | solution.py:13
  313.4 3.3 gather_fusion
  319.7 12.0 %collective-permute-done = bf16[2,512,256]{1,2,0:T(8,128)(2,1)S(1)} collective-permute-done((bf16[2,512,256]{1,2,0:T(8,128)(2,1)}, bf16[2,512,256]{1,2,0:T(8,128)(2,1)S(1)}, u32[]{:S(2)}, u32[]{:S(2)}) %collective-permute-start) | collective-permute-done | bytes 524320 | tf_op jit(solution)/shard_map/while/body/eval_jaxpr/ppermute | solution.py:13
  341.9 11.1 %collective-permute-done = bf16[2,512,256]{1,2,0:T(8,128)(2,1)S(1)} collective-permute-done((bf16[2,512,256]{1,2,0:T(8,128)(2,1)}, bf16[2,512,256]{1,2,0:T(8,128)(2,1)S(1)}, u32[]{:S(2)}, u32[]{:S(2)}) %collective-permute-start) | collective-permute-done | bytes 524320 | tf_op jit(solution)/shard_map/while/body/eval_jaxpr/ppermute | solution.py:13
  363.2 10.2 %collective-permute-done = bf16[2,512,256]{1,2,0:T(8,128)(2,1)S(1)} collective-permute-done((bf16[2,512,256]{1,2,0:T(8,128)(2,1)}, bf16[2,512,256]{1,2,0:T(8,128)(2,1)S(1)}, u32[]{:S(2)}, u32[]{:S(2)}) %collective-permute-start) | collective-permute-done | bytes 524320 | tf_op jit(solution)/shard_map/while/body/eval_jaxpr/ppermute | solution.py:13
  383.6 9.3 %collective-permute-done = bf16[2,512,256]{1,2,0:T(8,128)(2,1)S(1)} collective-permute-done((bf16[2,512,256]{1,2,0:T(8,128)(2,1)}, bf16[2,512,256]{1,2,0:T(8,128)(2,1)S(1)}, u32[]{:S(2)}, u32[]{:S(2)}) %collective-permute-start) | collective-permute-done | bytes 524320 | tf_op jit(solution)/shard_map/while/body/eval_jaxpr/ppermute | solution.py:13
  403.1 8.4 %collective-permute-done = bf16[2,512,256]{1,2,0:T(8,128)(2,1)S(1)} collective-permute-done((bf16[2,512,256]{1,2,0:T(8,128)(2,1)}, bf16[2,512,256]{1,2,0:T(8,128)(2,1)S(1)}, u32[]{:S(2)}, u32[]{:S(2)}) %collective-permute-start) | collective-permute-done | bytes 524320 | tf_op jit(solution)/shard_map/while/body/eval_jaxpr/ppermute | solution.py:13
  421.7 7.5 %collective-permute-done = bf16[2,512,256]{1,2,0:T(8,128)(2,1)S(1)} collective-permute-done((bf16[2,512,256]{1,2,0:T(8,128)(2,1)}, bf16[2,512,256]{1,2,0:T(8,128)(2,1)S(1)}, u32[]{:S(2)}, u32[]{:S(2)}) %collective-permute-start) | collective-permute-done | bytes 524320 | tf_op jit(solution)/shard_map/while/body/eval_jaxpr/ppermute | solution.py:13
  439.3 6.5 %collective-permute-done = bf16[2,512,256]{1,2,0:T(8,128)(2,1)S(1)} collective-permute-done((bf16[2,512,256]{1,2,0:T(8,128)(2,1)}, bf16[2,512,256]{1,2,0:T(8,128)(2,1)S(1)}, u32[]{:S(2)}, u32[]{:S(2)}) %collective-permute-start) | collective-permute-done | bytes 524320 | tf_op jit(solution)/shard_map/while/body/eval_jaxpr/ppermute | solution.py:13
  456.1 6.1 collective-permute-done
  472.4 6.1 collective-permute-done
  488.7 6.1 collective-permute-done
  505.0 6.1 collective-permute-done
  521.3 6.1 collective-permute-done
  537.6 6.4 collective-permute-done
  554.1 7.4 %collective-permute-done = bf16[2,512,256]{1,2,0:T(8,128)(2,1)S(1)} collective-permute-done((bf16[2,512,256]{1,2,0:T(8,128)(2,1)}, bf16[2,512,256]{1,2,0:T(8,128)(2,1)S(1)}, u32[]{:S(2)}, u32[]{:S(2)}) %collective-permute-start) | collective-permute-done | bytes 524320 | tf_op jit(solution)/shard_map/while/body/eval_jaxpr/ppermute | solution.py:13
  571.8 8.5 %collective-permute-done = bf16[2,512,256]{1,2,0:T(8,128)(2,1)S(1)} collective-permute-done((bf16[2,512,256]{1,2,0:T(8,128)(2,1)}, bf16[2,512,256]{1,2,0:T(8,128)(2,1)S(1)}, u32[]{:S(2)}, u32[]{:S(2)}) %collective-permute-start) | collective-permute-done | bytes 524320 | tf_op jit(solution)/shard_map/while/body/eval_jaxpr/ppermute | solution.py:13
  585.7 59.6 %reduce-scatter.2.cloned.1.call-done = bf16[512,256]{1,0:T(8,128)(2,1)} async-done(((bf16[512,1024]{1,0:T(8,128)(2,1)}), bf16[512,256]{1,0:T(8,128)(2,1)}) %reduce-scatter.2.cloned.1.call-update) | async-done | bytes 262160 | tf_op jit(solution)/shard_map/reduce_scatter | solution.py:86
  (580 shorter events, 281.4 us)
Async XLA Ops:
  6.5 8.9 %copy-start = (bf16[512,1024]{1,0:T(8,128)(2,1)S(1)}, bf16[512,1024]{1,0:T(8,128)(2,1)}, u32[]{:S(2)}) copy-start(bf16[512,1024]{1,0:T(8,128)(2,1)} %param.13) | copy-start | bytes 3145732
  6.5 10.4 %copy-start.2 = (bf16[1024,256]{1,0:T(8,128)(2,1)S(1)}, bf16[1024,256]{1,0:T(8,128)(2,1)}, u32[]{:S(2)}) copy-start(bf16[1024,256]{1,0:T(8,128)(2,1)} %param.15) | copy-start | bytes 1572868
  6.5 638.7 %reduce-scatter.2.cloned.1.call-start = ((), (), s32[]{:S(2)}) async-start(), calls=%async_computation.1 | async-start | bytes 1310720 | tf_op jit(solution)/shard_map/reduce_scatter | solution.py:86
  17.5 1.9 copy-start.3
  19.4 2.4 copy-start.1
  21.8 562.4 %copy-start.4 = (bf16[256,1024]{1,0:T(8,128)(2,1)S(1)}, bf16[256,1024]{1,0:T(8,128)(2,1)}, u32[]{:S(2)}) copy-start(bf16[256,1024]{1,0:T(8,128)(2,1)} %param.17) | copy-start | bytes 1572868
  21.8 19.8 %collective-permute-start = (bf16[2,512,256]{1,2,0:T(8,128)(2,1)}, bf16[2,512,256]{1,2,0:T(8,128)(2,1)S(1)}, u32[]{:S(2)}, u32[]{:S(2)}) collective-permute-start(bf16[2,512,256]{1,2,0:T(8,128)(2,1)} %get-tuple-element.374), channel_id=1, source_target_pairs={{0,4},{4,8},{8,12},{12,16},{16,20},{20,24},{24,28},{28,32},{32,36}... | collective-permute-start | bytes 1572872 | tf_op jit(solution)/shard_map/while/body/eval_jaxpr/ppermute | solution.py:13
  45.4 16.6 %collective-permute-start = (bf16[2,512,256]{1,2,0:T(8,128)(2,1)}, bf16[2,512,256]{1,2,0:T(8,128)(2,1)S(1)}, u32[]{:S(2)}, u32[]{:S(2)}) collective-permute-start(bf16[2,512,256]{1,2,0:T(8,128)(2,1)} %get-tuple-element.374), channel_id=1, source_target_pairs={{0,4},{4,8},{8,12},{12,16},{16,20},{20,24},{24,28},{28,32},{32,36}... | collective-permute-start | bytes 1572872 | tf_op jit(solution)/shard_map/while/body/eval_jaxpr/ppermute | solution.py:13
  65.9 15.7 %collective-permute-start = (bf16[2,512,256]{1,2,0:T(8,128)(2,1)}, bf16[2,512,256]{1,2,0:T(8,128)(2,1)S(1)}, u32[]{:S(2)}, u32[]{:S(2)}) collective-permute-start(bf16[2,512,256]{1,2,0:T(8,128)(2,1)} %get-tuple-element.374), channel_id=1, source_target_pairs={{0,4},{4,8},{8,12},{12,16},{16,20},{20,24},{24,28},{28,32},{32,36}... | collective-permute-start | bytes 1572872 | tf_op jit(solution)/shard_map/while/body/eval_jaxpr/ppermute | solution.py:13
  85.4 14.8 %collective-permute-start = (bf16[2,512,256]{1,2,0:T(8,128)(2,1)}, bf16[2,512,256]{1,2,0:T(8,128)(2,1)S(1)}, u32[]{:S(2)}, u32[]{:S(2)}) collective-permute-start(bf16[2,512,256]{1,2,0:T(8,128)(2,1)} %get-tuple-element.374), channel_id=1, source_target_pairs={{0,4},{4,8},{8,12},{12,16},{16,20},{20,24},{24,28},{28,32},{32,36}... | collective-permute-start | bytes 1572872 | tf_op jit(solution)/shard_map/while/body/eval_jaxpr/ppermute | solution.py:13
  104.0 13.9 %collective-permute-start = (bf16[2,512,256]{1,2,0:T(8,128)(2,1)}, bf16[2,512,256]{1,2,0:T(8,128)(2,1)S(1)}, u32[]{:S(2)}, u32[]{:S(2)}) collective-permute-start(bf16[2,512,256]{1,2,0:T(8,128)(2,1)} %get-tuple-element.374), channel_id=1, source_target_pairs={{0,4},{4,8},{8,12},{12,16},{16,20},{20,24},{24,28},{28,32},{32,36}... | collective-permute-start | bytes 1572872 | tf_op jit(solution)/shard_map/while/body/eval_jaxpr/ppermute | solution.py:13
  121.7 12.9 %collective-permute-start = (bf16[2,512,256]{1,2,0:T(8,128)(2,1)}, bf16[2,512,256]{1,2,0:T(8,128)(2,1)S(1)}, u32[]{:S(2)}, u32[]{:S(2)}) collective-permute-start(bf16[2,512,256]{1,2,0:T(8,128)(2,1)} %get-tuple-element.374), channel_id=1, source_target_pairs={{0,4},{4,8},{8,12},{12,16},{16,20},{20,24},{24,28},{28,32},{32,36}... | collective-permute-start | bytes 1572872 | tf_op jit(solution)/shard_map/while/body/eval_jaxpr/ppermute | solution.py:13
  138.5 12.5 %collective-permute-start = (bf16[2,512,256]{1,2,0:T(8,128)(2,1)}, bf16[2,512,256]{1,2,0:T(8,128)(2,1)S(1)}, u32[]{:S(2)}, u32[]{:S(2)}) collective-permute-start(bf16[2,512,256]{1,2,0:T(8,128)(2,1)} %get-tuple-element.374), channel_id=1, source_target_pairs={{0,4},{4,8},{8,12},{12,16},{16,20},{20,24},{24,28},{28,32},{32,36}... | collective-permute-start | bytes 1572872 | tf_op jit(solution)/shard_map/while/body/eval_jaxpr/ppermute | solution.py:13
  154.8 12.5 %collective-permute-start = (bf16[2,512,256]{1,2,0:T(8,128)(2,1)}, bf16[2,512,256]{1,2,0:T(8,128)(2,1)S(1)}, u32[]{:S(2)}, u32[]{:S(2)}) collective-permute-start(bf16[2,512,256]{1,2,0:T(8,128)(2,1)} %get-tuple-element.374), channel_id=1, source_target_pairs={{0,4},{4,8},{8,12},{12,16},{16,20},{20,24},{24,28},{28,32},{32,36}... | collective-permute-start | bytes 1572872 | tf_op jit(solution)/shard_map/while/body/eval_jaxpr/ppermute | solution.py:13
  171.1 12.5 %collective-permute-start = (bf16[2,512,256]{1,2,0:T(8,128)(2,1)}, bf16[2,512,256]{1,2,0:T(8,128)(2,1)S(1)}, u32[]{:S(2)}, u32[]{:S(2)}) collective-permute-start(bf16[2,512,256]{1,2,0:T(8,128)(2,1)} %get-tuple-element.374), channel_id=1, source_target_pairs={{0,4},{4,8},{8,12},{12,16},{16,20},{20,24},{24,28},{28,32},{32,36}... | collective-permute-start | bytes 1572872 | tf_op jit(solution)/shard_map/while/body/eval_jaxpr/ppermute | solution.py:13
  187.4 12.5 %collective-permute-start = (bf16[2,512,256]{1,2,0:T(8,128)(2,1)}, bf16[2,512,256]{1,2,0:T(8,128)(2,1)S(1)}, u32[]{:S(2)}, u32[]{:S(2)}) collective-permute-start(bf16[2,512,256]{1,2,0:T(8,128)(2,1)} %get-tuple-element.374), channel_id=1, source_target_pairs={{0,4},{4,8},{8,12},{12,16},{16,20},{20,24},{24,28},{28,32},{32,36}... | collective-permute-start | bytes 1572872 | tf_op jit(solution)/shard_map/while/body/eval_jaxpr/ppermute | solution.py:13
  203.7 12.5 %collective-permute-start = (bf16[2,512,256]{1,2,0:T(8,128)(2,1)}, bf16[2,512,256]{1,2,0:T(8,128)(2,1)S(1)}, u32[]{:S(2)}, u32[]{:S(2)}) collective-permute-start(bf16[2,512,256]{1,2,0:T(8,128)(2,1)} %get-tuple-element.374), channel_id=1, source_target_pairs={{0,4},{4,8},{8,12},{12,16},{16,20},{20,24},{24,28},{28,32},{32,36}... | collective-permute-start | bytes 1572872 | tf_op jit(solution)/shard_map/while/body/eval_jaxpr/ppermute | solution.py:13
  220.0 12.7 %collective-permute-start = (bf16[2,512,256]{1,2,0:T(8,128)(2,1)}, bf16[2,512,256]{1,2,0:T(8,128)(2,1)S(1)}, u32[]{:S(2)}, u32[]{:S(2)}) collective-permute-start(bf16[2,512,256]{1,2,0:T(8,128)(2,1)} %get-tuple-element.374), channel_id=1, source_target_pairs={{0,4},{4,8},{8,12},{12,16},{16,20},{20,24},{24,28},{28,32},{32,36}... | collective-permute-start | bytes 1572872 | tf_op jit(solution)/shard_map/while/body/eval_jaxpr/ppermute | solution.py:13
  236.5 13.8 %collective-permute-start = (bf16[2,512,256]{1,2,0:T(8,128)(2,1)}, bf16[2,512,256]{1,2,0:T(8,128)(2,1)S(1)}, u32[]{:S(2)}, u32[]{:S(2)}) collective-permute-start(bf16[2,512,256]{1,2,0:T(8,128)(2,1)} %get-tuple-element.374), channel_id=1, source_target_pairs={{0,4},{4,8},{8,12},{12,16},{16,20},{20,24},{24,28},{28,32},{32,36}... | collective-permute-start | bytes 1572872 | tf_op jit(solution)/shard_map/while/body/eval_jaxpr/ppermute | solution.py:13
  254.1 14.8 %collective-permute-start = (bf16[2,512,256]{1,2,0:T(8,128)(2,1)}, bf16[2,512,256]{1,2,0:T(8,128)(2,1)S(1)}, u32[]{:S(2)}, u32[]{:S(2)}) collective-permute-start(bf16[2,512,256]{1,2,0:T(8,128)(2,1)} %get-tuple-element.374), channel_id=1, source_target_pairs={{0,4},{4,8},{8,12},{12,16},{16,20},{20,24},{24,28},{28,32},{32,36}... | collective-permute-start | bytes 1572872 | tf_op jit(solution)/shard_map/while/body/eval_jaxpr/ppermute | solution.py:13
  272.8 15.9 %collective-permute-start = (bf16[2,512,256]{1,2,0:T(8,128)(2,1)}, bf16[2,512,256]{1,2,0:T(8,128)(2,1)S(1)}, u32[]{:S(2)}, u32[]{:S(2)}) collective-permute-start(bf16[2,512,256]{1,2,0:T(8,128)(2,1)} %get-tuple-element.374), channel_id=1, source_target_pairs={{0,4},{4,8},{8,12},{12,16},{16,20},{20,24},{24,28},{28,32},{32,36}... | collective-permute-start | bytes 1572872 | tf_op jit(solution)/shard_map/while/body/eval_jaxpr/ppermute | solution.py:13
  292.5 17.0 %collective-permute-start = (bf16[2,512,256]{1,2,0:T(8,128)(2,1)}, bf16[2,512,256]{1,2,0:T(8,128)(2,1)S(1)}, u32[]{:S(2)}, u32[]{:S(2)}) collective-permute-start(bf16[2,512,256]{1,2,0:T(8,128)(2,1)} %get-tuple-element.374), channel_id=1, source_target_pairs={{0,4},{4,8},{8,12},{12,16},{16,20},{20,24},{24,28},{28,32},{32,36}... | collective-permute-start | bytes 1572872 | tf_op jit(solution)/shard_map/while/body/eval_jaxpr/ppermute | solution.py:13
  313.3 18.3 %collective-permute-start = (bf16[2,512,256]{1,2,0:T(8,128)(2,1)}, bf16[2,512,256]{1,2,0:T(8,128)(2,1)S(1)}, u32[]{:S(2)}, u32[]{:S(2)}) collective-permute-start(bf16[2,512,256]{1,2,0:T(8,128)(2,1)} %get-tuple-element.374), channel_id=1, source_target_pairs={{0,4},{4,8},{8,12},{12,16},{16,20},{20,24},{24,28},{28,32},{32,36}... | collective-permute-start | bytes 1572872 | tf_op jit(solution)/shard_map/while/body/eval_jaxpr/ppermute | solution.py:13
  335.5 17.5 %collective-permute-start = (bf16[2,512,256]{1,2,0:T(8,128)(2,1)}, bf16[2,512,256]{1,2,0:T(8,128)(2,1)S(1)}, u32[]{:S(2)}, u32[]{:S(2)}) collective-permute-start(bf16[2,512,256]{1,2,0:T(8,128)(2,1)} %get-tuple-element.374), channel_id=1, source_target_pairs={{0,4},{4,8},{8,12},{12,16},{16,20},{20,24},{24,28},{28,32},{32,36}... | collective-permute-start | bytes 1572872 | tf_op jit(solution)/shard_map/while/body/eval_jaxpr/ppermute | solution.py:13
  356.8 16.6 %collective-permute-start = (bf16[2,512,256]{1,2,0:T(8,128)(2,1)}, bf16[2,512,256]{1,2,0:T(8,128)(2,1)S(1)}, u32[]{:S(2)}, u32[]{:S(2)}) collective-permute-start(bf16[2,512,256]{1,2,0:T(8,128)(2,1)} %get-tuple-element.374), channel_id=1, source_target_pairs={{0,4},{4,8},{8,12},{12,16},{16,20},{20,24},{24,28},{28,32},{32,36}... | collective-permute-start | bytes 1572872 | tf_op jit(solution)/shard_map/while/body/eval_jaxpr/ppermute | solution.py:13
  377.3 15.7 %collective-permute-start = (bf16[2,512,256]{1,2,0:T(8,128)(2,1)}, bf16[2,512,256]{1,2,0:T(8,128)(2,1)S(1)}, u32[]{:S(2)}, u32[]{:S(2)}) collective-permute-start(bf16[2,512,256]{1,2,0:T(8,128)(2,1)} %get-tuple-element.374), channel_id=1, source_target_pairs={{0,4},{4,8},{8,12},{12,16},{16,20},{20,24},{24,28},{28,32},{32,36}... | collective-permute-start | bytes 1572872 | tf_op jit(solution)/shard_map/while/body/eval_jaxpr/ppermute | solution.py:13
  396.7 14.7 %collective-permute-start = (bf16[2,512,256]{1,2,0:T(8,128)(2,1)}, bf16[2,512,256]{1,2,0:T(8,128)(2,1)S(1)}, u32[]{:S(2)}, u32[]{:S(2)}) collective-permute-start(bf16[2,512,256]{1,2,0:T(8,128)(2,1)} %get-tuple-element.374), channel_id=1, source_target_pairs={{0,4},{4,8},{8,12},{12,16},{16,20},{20,24},{24,28},{28,32},{32,36}... | collective-permute-start | bytes 1572872 | tf_op jit(solution)/shard_map/while/body/eval_jaxpr/ppermute | solution.py:13
  415.3 13.8 %collective-permute-start = (bf16[2,512,256]{1,2,0:T(8,128)(2,1)}, bf16[2,512,256]{1,2,0:T(8,128)(2,1)S(1)}, u32[]{:S(2)}, u32[]{:S(2)}) collective-permute-start(bf16[2,512,256]{1,2,0:T(8,128)(2,1)} %get-tuple-element.374), channel_id=1, source_target_pairs={{0,4},{4,8},{8,12},{12,16},{16,20},{20,24},{24,28},{28,32},{32,36}... | collective-permute-start | bytes 1572872 | tf_op jit(solution)/shard_map/while/body/eval_jaxpr/ppermute | solution.py:13
  433.0 12.9 %collective-permute-start = (bf16[2,512,256]{1,2,0:T(8,128)(2,1)}, bf16[2,512,256]{1,2,0:T(8,128)(2,1)S(1)}, u32[]{:S(2)}, u32[]{:S(2)}) collective-permute-start(bf16[2,512,256]{1,2,0:T(8,128)(2,1)} %get-tuple-element.374), channel_id=1, source_target_pairs={{0,4},{4,8},{8,12},{12,16},{16,20},{20,24},{24,28},{28,32},{32,36}... | collective-permute-start | bytes 1572872 | tf_op jit(solution)/shard_map/while/body/eval_jaxpr/ppermute | solution.py:13
  449.7 12.5 %collective-permute-start = (bf16[2,512,256]{1,2,0:T(8,128)(2,1)}, bf16[2,512,256]{1,2,0:T(8,128)(2,1)S(1)}, u32[]{:S(2)}, u32[]{:S(2)}) collective-permute-start(bf16[2,512,256]{1,2,0:T(8,128)(2,1)} %get-tuple-element.374), channel_id=1, source_target_pairs={{0,4},{4,8},{8,12},{12,16},{16,20},{20,24},{24,28},{28,32},{32,36}... | collective-permute-start | bytes 1572872 | tf_op jit(solution)/shard_map/while/body/eval_jaxpr/ppermute | solution.py:13
  466.0 12.5 %collective-permute-start = (bf16[2,512,256]{1,2,0:T(8,128)(2,1)}, bf16[2,512,256]{1,2,0:T(8,128)(2,1)S(1)}, u32[]{:S(2)}, u32[]{:S(2)}) collective-permute-start(bf16[2,512,256]{1,2,0:T(8,128)(2,1)} %get-tuple-element.374), channel_id=1, source_target_pairs={{0,4},{4,8},{8,12},{12,16},{16,20},{20,24},{24,28},{28,32},{32,36}... | collective-permute-start | bytes 1572872 | tf_op jit(solution)/shard_map/while/body/eval_jaxpr/ppermute | solution.py:13
  482.3 12.5 %collective-permute-start = (bf16[2,512,256]{1,2,0:T(8,128)(2,1)}, bf16[2,512,256]{1,2,0:T(8,128)(2,1)S(1)}, u32[]{:S(2)}, u32[]{:S(2)}) collective-permute-start(bf16[2,512,256]{1,2,0:T(8,128)(2,1)} %get-tuple-element.374), channel_id=1, source_target_pairs={{0,4},{4,8},{8,12},{12,16},{16,20},{20,24},{24,28},{28,32},{32,36}... | collective-permute-start | bytes 1572872 | tf_op jit(solution)/shard_map/while/body/eval_jaxpr/ppermute | solution.py:13
  498.6 12.5 %collective-permute-start = (bf16[2,512,256]{1,2,0:T(8,128)(2,1)}, bf16[2,512,256]{1,2,0:T(8,128)(2,1)S(1)}, u32[]{:S(2)}, u32[]{:S(2)}) collective-permute-start(bf16[2,512,256]{1,2,0:T(8,128)(2,1)} %get-tuple-element.374), channel_id=1, source_target_pairs={{0,4},{4,8},{8,12},{12,16},{16,20},{20,24},{24,28},{28,32},{32,36}... | collective-permute-start | bytes 1572872 | tf_op jit(solution)/shard_map/while/body/eval_jaxpr/ppermute | solution.py:13
  514.9 12.5 %collective-permute-start = (bf16[2,512,256]{1,2,0:T(8,128)(2,1)}, bf16[2,512,256]{1,2,0:T(8,128)(2,1)S(1)}, u32[]{:S(2)}, u32[]{:S(2)}) collective-permute-start(bf16[2,512,256]{1,2,0:T(8,128)(2,1)} %get-tuple-element.374), channel_id=1, source_target_pairs={{0,4},{4,8},{8,12},{12,16},{16,20},{20,24},{24,28},{28,32},{32,36}... | collective-permute-start | bytes 1572872 | tf_op jit(solution)/shard_map/while/body/eval_jaxpr/ppermute | solution.py:13
  531.2 12.7 %collective-permute-start = (bf16[2,512,256]{1,2,0:T(8,128)(2,1)}, bf16[2,512,256]{1,2,0:T(8,128)(2,1)S(1)}, u32[]{:S(2)}, u32[]{:S(2)}) collective-permute-start(bf16[2,512,256]{1,2,0:T(8,128)(2,1)} %get-tuple-element.374), channel_id=1, source_target_pairs={{0,4},{4,8},{8,12},{12,16},{16,20},{20,24},{24,28},{28,32},{32,36}... | collective-permute-start | bytes 1572872 | tf_op jit(solution)/shard_map/while/body/eval_jaxpr/ppermute | solution.py:13
  547.8 13.8 %collective-permute-start = (bf16[2,512,256]{1,2,0:T(8,128)(2,1)}, bf16[2,512,256]{1,2,0:T(8,128)(2,1)S(1)}, u32[]{:S(2)}, u32[]{:S(2)}) collective-permute-start(bf16[2,512,256]{1,2,0:T(8,128)(2,1)} %get-tuple-element.374), channel_id=1, source_target_pairs={{0,4},{4,8},{8,12},{12,16},{16,20},{20,24},{24,28},{28,32},{32,36}... | collective-permute-start | bytes 1572872 | tf_op jit(solution)/shard_map/while/body/eval_jaxpr/ppermute | solution.py:13
  565.4 14.9 %collective-permute-start = (bf16[2,512,256]{1,2,0:T(8,128)(2,1)}, bf16[2,512,256]{1,2,0:T(8,128)(2,1)S(1)}, u32[]{:S(2)}, u32[]{:S(2)}) collective-permute-start(bf16[2,512,256]{1,2,0:T(8,128)(2,1)} %get-tuple-element.374), channel_id=1, source_target_pairs={{0,4},{4,8},{8,12},{12,16},{16,20},{20,24},{24,28},{28,32},{32,36}... | collective-permute-start | bytes 1572872 | tf_op jit(solution)/shard_map/while/body/eval_jaxpr/ppermute | solution.py:13
Sparse Core Ops, SparseCore 0:
  585.8 59.4 reduce-scatter.1
where the time goes:
time: 652 us
  waiting for transfers between devices  304 us (47%)
  local copies, waits for them, and re-layouts  223 us (34%)
  matrix products  68.9 us (11%)
  other arithmetic  37.6 us (6%)
  between operations  13.5 us (2%)
    ppermute x31, waiting for transfers between devices, from_behind(): return lax.ppermute(value, axis, pairs)  244 us
    gather x32, local copies, waits for them, and re-layouts, key_mask(): key_orig = jnp.take(block_order, key_blocks)  107 us
    reduce_scatter x1, waiting for transfers between devices, body(): lax.psum_scatter(partial_out.astype(jnp.bfloat16), 'head', scatter_dimens...  59.6 us
    broadcast_in_dim x32, local copies, waits for them, and re-layouts, key_mask(): return jnp.repeat(block_cols, BLOCK, axis=0) > 0  51.1 us
    dot_general x32, matrix products, attend(): jnp.einsum('hqk,khd->qhd', probs.astype(jnp.bfloat16), value_heads, prefe...  35.7 us
    gather x32, local copies, waits for them, and re-layouts, key_mask(): block_cols = jnp.take(mask_rows, key_orig, axis=1)  33.2 us
    dot_general x32, matrix products, attend(): jnp.einsum('qhd,khd->hqk', query_heads, key_heads, preferred_element_type...  29.3 us
    reduce_sum x32, other arithmetic, attend(): row_sum = row_sum * factor + jnp.sum(probs, axis=2)  28.9 us
  transfers between devices with their start and end apart: 32, of which 32 were waited for; matrix products, arithmetic and copies ran while one was open for 30% of the time, Pallas kernels for 0%

commit v1 on v0

v1 whole, which is shorter than its diff:
```python
import functools

import jax
import jax.numpy as jnp
from jax import lax
from jax.experimental import pallas as pl
from jax.experimental.pallas import tpu as pltpu
from jax.sharding import PartitionSpec as P

HEAD_DIM = 64
BLOCK = 128
NB = 128
ROWS = 512
NY, NZ = 4, 4
LIST_PAD = -1e30
MESH = pl.DeviceIdType.MESH
BF16 = jnp.bfloat16
F32 = jnp.float32


def place():
    ctx = lax.axis_index("ctx")
    head = lax.axis_index("head")
    return ctx // 8, (ctx // 2) % 4, ctx % 2, head // 2, head % 2


def ctx_of(y, z, x_lo):
    return (y * NZ + z) * 2 + x_lo


def project_kernel(tok_ref, wq_ref, wk_ref, wv_ref, mask_ref, order_row_ref, kv_ref, q_ref, lists_ref):
    tok = tok_ref[...]
    keys = jnp.dot(tok, wk_ref[...], preferred_element_type=F32).astype(BF16)
    vals = jnp.dot(tok, wv_ref[...], preferred_element_type=F32).astype(BF16)
    query = jnp.dot(tok, wq_ref[...], preferred_element_type=F32).astype(BF16)
    half = ROWS // 2
    for j in range(4):
        cols = slice(j * HEAD_DIM, (j + 1) * HEAD_DIM)
        kv_ref[j] = jnp.concatenate([keys[:, cols], vals[:, cols]], axis=1)
        q_ref[j] = jnp.concatenate([query[:half, cols], query[half:, cols]], axis=1)

    _, z, _, _, core = place()
    sub = lax.broadcasted_iota(jnp.int32, (NB, NB), 0)
    lane = lax.broadcasted_iota(jnp.int32, (NB, NB), 1)
    initial_of = (order_row_ref[...] == sub).astype(F32).astype(BF16)
    i16 = lax.broadcasted_iota(jnp.int32, (16, NB), 0)
    l16 = lax.broadcasted_iota(jnp.int32, (16, NB), 1)
    mine = ((i16 // 4 * NZ + z) * 2 + core) * 4 + i16 % 4
    row_pick = (l16 == mine).astype(F32).astype(BF16)
    rows_initial = lax.dot_general(
        row_pick, initial_of, (((1,), (1,)), ((), ())), preferred_element_type=F32
    ).astype(BF16)
    mask = mask_ref[...].astype(F32).astype(BF16)
    mask_rows = jnp.dot(rows_initial, mask, preferred_element_type=F32).astype(BF16)
    allowed = jnp.dot(mask_rows, initial_of, preferred_element_type=F32)
    before = (sub < lane).astype(F32).astype(BF16)
    rank = jnp.dot(allowed.astype(BF16), before, preferred_element_type=F32)
    rank = jnp.where(allowed > 0.5, rank, -1.0)
    lane_row = lax.broadcasted_iota(jnp.int32, (8, NB), 1).astype(F32).astype(BF16)
    sub_f = sub.astype(F32)
    for i in range(16):
        hot = (rank[i : i + 1, :] == sub_f).astype(F32).astype(BF16)
        got = lax.dot_general(lane_row, hot, (((1,), (1,)), ((), ())), preferred_element_type=F32)
        lists_ref[i : i + 1, :] = got[0:1, :].astype(jnp.int32)
    count = jnp.sum(allowed, axis=1, keepdims=True)
    lists_ref[16:32, :] = jnp.broadcast_to(count, (16, NB)).astype(jnp.int32)


def project(tokens, w_query, w_key, w_value, block_mask, order_row):
    whole = pl.BlockSpec(memory_space=pltpu.VMEM)
    return pl.pallas_call(
        project_kernel,
        out_shape=(
            jax.ShapeDtypeStruct((4, ROWS, 128), BF16),
            jax.ShapeDtypeStruct((4, ROWS // 2, 128), BF16),
            jax.ShapeDtypeStruct((32, NB), jnp.int32),
        ),
        in_specs=[whole] * 6,
        out_specs=(whole, whole, whole),
        name="project",
    )(tokens, w_query, w_key, w_value, block_mask, order_row)


def exchange_kernel(kv_ref, q_ref, w_ref, kv_all, q_all, w_all, a_send, a_recv, q_send, q_recv, w_send, w_recv,
                    z_send, z_recv, c_send, c_recv):
    y, z, x_lo, x_hi, core = place()
    me_ctx = ctx_of(y, z, x_lo)
    me_head = x_hi * 2 + core
    swap_head = x_hi * 2 + x_lo
    stays = x_lo == core
    up = (ctx_of(y, (z + 1) % NZ, x_lo), me_head)
    down = (ctx_of(y, (z + 3) % NZ, x_lo), me_head)
    twin = (me_ctx, x_hi * 2 + 1 - core)
    head_peers = [(me_ctx, (me_head + k) % 4) for k in range(1, 4)]
    a_to = [(ctx_of((y + d) % NY, z, core), swap_head) for d in range(4)]

    barrier = pltpu.get_barrier_semaphore()
    for peer in [up, down, *head_peers, *a_to[1:]]:
        pl.semaphore_signal(barrier, inc=1, device_id=peer, device_id_type=MESH)

    @pl.when(jnp.logical_not(stays))
    def _():
        pl.semaphore_signal(barrier, inc=1, device_id=a_to[0], device_id_type=MESH)

    pl.semaphore_wait(barrier, 8 + (x_lo + core) % 2)

    def remote(src, dst, send_sem, recv_sem, device):
        return pltpu.make_async_remote_copy(
            src_ref=src, dst_ref=dst, send_sem=send_sem, recv_sem=recv_sem, device_id=device, device_id_type=MESH
        )

    sent = []

    def send(src, dst, send_sem, recv_sem, device):
        copy = remote(src, dst, send_sem, recv_sem, device)
        copy.start()
        sent.append(copy)

    def arrived(dst, send_sem, recv_sem, device):
        remote(dst, dst, send_sem, recv_sem, device).wait_recv()

    own = y % NY
    kv_here = remote(kv_ref.at[own], kv_all.at[me_ctx], a_send.at[0], a_recv.at[0], a_to[0])
    q_here = remote(q_ref.at[own], q_all.at[y], q_send.at[0], q_recv.at[0], a_to[0])
    kv_local = pltpu.make_async_copy(kv_ref.at[own], kv_all.at[me_ctx], a_recv.at[0])
    q_local = pltpu.make_async_copy(q_ref.at[own], q_all.at[y], q_recv.at[0])

    @pl.when(stays)
    def _():
        kv_local.start()
        q_local.start()

    @pl.when(jnp.logical_not(stays))
    def _():
        kv_here.start()
        q_here.start()

    order = (1, 3, 2)
    for d in order:
        send(kv_ref.at[(y + d) % NY], kv_all.at[me_ctx], a_send.at[d], a_recv.at[d], a_to[d])
    for d in order:
        send(q_ref.at[(y + d) % NY], q_all.at[y], q_send.at[d], q_recv.at[d], a_to[d])
    for k in range(1, 4):
        to = (me_head + k) % 4
        send(w_ref.at[:, pl.ds(pl.multiple_of(to * 256, 256), 256)], w_all.at[me_head], w_send.at[k - 1], w_recv.at[k - 1],
             head_peers[k - 1])
    w_local = pltpu.make_async_copy(
        w_ref.at[:, pl.ds(pl.multiple_of(me_head * 256, 256), 256)], w_all.at[me_head], w_recv.at[3]
    )
    w_local.start()

    def chunk(d, dz):
        return kv_all.at[ctx_of((y + NY - d) % NY, (z + NZ + dz) % NZ, core)]

    for d in (0, 1, 3, 2):
        if d == 0:
            @pl.when(stays)
            def _():
                kv_local.wait()

            @pl.when(jnp.logical_not(stays))
            def _():
                kv_here.wait_recv()
        else:
            arrived(chunk(d, 0), a_send.at[d], a_recv.at[d], a_to[d])
        send(chunk(d, 0), chunk(d, 0), z_send.at[d], z_recv.at[d], up)
        send(chunk(d, 0), chunk(d, 0), z_send.at[4 + d], z_recv.at[4 + d], down)
        send(chunk(d, 0), chunk(d, 0), c_send.at[d], c_recv.at[d], twin)
    for d in (0, 1, 3, 2):
        below, above = chunk(d, -1), chunk(d, 1)
        arrived(below, z_send.at[d], z_recv.at[d], up)
        if d in (0, 1):
            send(below, below, z_send.at[8 + d], z_recv.at[8 + d], up)
        send(below, below, c_send.at[4 + d], c_recv.at[4 + d], twin)
        arrived(above, z_send.at[4 + d], z_recv.at[4 + d], down)
        if d in (2, 3):
            send(above, above, z_send.at[8 + d], z_recv.at[8 + d], down)
        send(above, above, c_send.at[8 + d], c_recv.at[8 + d], twin)
    for d in (0, 1, 3, 2):
        far = chunk(d, 2)
        arrived(far, z_send.at[8 + d], z_recv.at[8 + d], up)
        send(far, far, c_send.at[12 + d], c_recv.at[12 + d], twin)

    def twin_chunk(d, dz):
        return kv_all.at[ctx_of((y + NY - d) % NY, (z + NZ + dz) % NZ, 1 - core)]

    for place_of, dz in ((0, 0), (4, -1), (8, 1), (12, 2)):
        for d in (0, 1, 3, 2):
            arrived(twin_chunk(d, dz), c_send.at[place_of + d], c_recv.at[place_of + d], twin)

    @pl.when(stays)
    def _():
        q_local.wait()

    @pl.when(jnp.logical_not(stays))
    def _():
        q_here.wait_recv()
        kv_here.wait_send()
        q_here.wait_send()

    for d in order:
        arrived(q_all.at[(y + NY - d) % NY], q_send.at[d], q_recv.at[d], a_to[d])
    for k in range(1, 4):
        arrived(w_all.at[(me_head + 4 - k) % 4], w_send.at[k - 1], w_recv.at[k - 1], head_peers[k - 1])
    w_local.wait()
    for copy in sent:
        copy.wait_send()


def exchange(kv, query, w_out):
    anywhere = pl.BlockSpec(memory_space=pl.ANY)
    dma = pltpu.SemaphoreType.DMA
    return pl.pallas_call(
        exchange_kernel,
        out_shape=(
            jax.ShapeDtypeStruct((32, ROWS, 128), BF16),
            jax.ShapeDtypeStruct((4, ROWS // 2, 128), BF16),
            jax.ShapeDtypeStruct((4, 256, 256), BF16),
        ),
        in_specs=[anywhere] * 3,
        out_specs=(anywhere,) * 3,
        scratch_shapes=[
            dma((4,)), dma((4,)), dma((4,)), dma((4,)), dma((4,)), dma((4,)),
            dma((12,)), dma((12,)), dma((16,)), dma((16,)),
        ],
        compiler_params=pltpu.CompilerParams(collective_id=0, has_side_effects=True),
        name="exchange",
    )(kv, query, w_out)


UNROLL = 4
EXP2_SCALE = (HEAD_DIM ** -0.5) * 1.4426950408889634


def attend_kernel(lists, q_ref, kv_ref, out_ref, qz, scores):
    lanes = lax.broadcasted_iota(jnp.int32, (BLOCK, 128), 1)
    nt = (((1,), (1,)), ((), ()))

    def owner(step, _):
        for b in range(4):
            row0 = (b % 2) * BLOCK
            q = q_ref[step, row0 : row0 + BLOCK, :]
            if b // 2:
                q = jnp.concatenate([q[:, HEAD_DIM:], q[:, :HEAD_DIM]], axis=1)
            qz[b] = jnp.where(lanes < HEAD_DIM, q, jnp.zeros_like(q))
        for b in range(4):
            i = step * 4 + b
            n = lists[16 + i, 0]
            groups = (n + UNROLL - 1) // UNROLL
            q = qz[b]

            def keys_at(k):
                start = pl.multiple_of(lists[i, k] * BLOCK, BLOCK)
                return kv_ref[pl.ds(start, BLOCK), :]

            def first(g, top):
                for u in range(UNROLL):
                    k = g * UNROLL + u
                    bias = jnp.where(k < n, 0.0, LIST_PAD).astype(F32)
                    s = lax.dot_general(q, keys_at(k), nt, preferred_element_type=F32) + bias
                    scores[k] = s
                    top = jnp.maximum(top, s)
                return top

            top = lax.fori_loop(0, groups, first, jnp.full((BLOCK, BLOCK), -3e38, F32))
            top = jnp.max(top, axis=1, keepdims=True)

            def second(g, carry):
                total, acc = carry
                probs, blocks = [], []
                for u in range(UNROLL):
                    k = g * UNROLL + u
                    p = jnp.exp2((scores[k] - top) * EXP2_SCALE)
                    total = total + p
                    probs.append(p.astype(BF16))
                    blocks.append(keys_at(k))
                acc = acc + jnp.dot(
                    jnp.concatenate(probs, axis=1), jnp.concatenate(blocks, axis=0), preferred_element_type=F32
                )
                return total, acc

            zero = jnp.zeros((BLOCK, 128), F32)
            total, acc = lax.fori_loop(0, groups, second, (zero, zero))
            denom = jnp.sum(total, axis=1, keepdims=True)
            row0, col0 = (b % 2) * BLOCK, (b // 2) * HEAD_DIM
            out_ref[step, row0 : row0 + BLOCK, col0 : col0 + HEAD_DIM] = (acc[:, HEAD_DIM:] / denom).astype(BF16)
        return 0

    lax.fori_loop(0, 4, owner, 0)


def attend(lists, query, kv):
    whole = pl.BlockSpec(memory_space=pltpu.VMEM)
    return pl.pallas_call(
        attend_kernel,
        out_shape=jax.ShapeDtypeStruct((4, ROWS // 2, 128), BF16),
        grid_spec=pltpu.PrefetchScalarGridSpec(
            num_scalar_prefetch=1,
            grid=(),
            in_specs=[whole, whole],
            out_specs=whole,
            scratch_shapes=[pltpu.VMEM((4, BLOCK, 128), BF16), pltpu.VMEM((NB, BLOCK, BLOCK), F32)],
        ),
        compiler_params=pltpu.CompilerParams(vmem_limit_bytes=32 << 20),
        name="attend",
    )(lists, query, kv)


def return_kernel(att_ref, all_ref, send_sems, recv_sems, c_send, c_recv):
    y, z, x_lo, x_hi, core = place()
    me_ctx = ctx_of(y, z, x_lo)
    stays = x_lo == core
    twin = (me_ctx, x_hi * 2 + 1 - core)
    me_global = (x_hi * 2 + x_lo) * 4 + y
    near = [(ctx_of((y + d) % NY, z, core), x_hi * 2 + x_lo) for d in range(4)]
    cross = [(ctx_of((y + d) % NY, z, core), (1 - x_hi) * 2 + x_lo) for d in range(4)]

    barrier = pltpu.get_barrier_semaphore()
    for peer in [twin, *cross, *near[1:]]:
        pl.semaphore_signal(barrier, inc=1, device_id=peer, device_id_type=MESH)

    @pl.when(jnp.logical_not(stays))
    def _():
        pl.semaphore_signal(barrier, inc=1, device_id=near[0], device_id_type=MESH)

    pl.semaphore_wait(barrier, 8 + (x_lo + core) % 2)

    def remote(src, dst, send_sem, recv_sem, device):
        return pltpu.make_async_remote_copy(
            src_ref=src, dst_ref=dst, send_sem=send_sem, recv_sem=recv_sem, device_id=device, device_id_type=MESH
        )

    sent = []

    def send(src, dst, send_sem, recv_sem, device):
        copy = remote(src, dst, send_sem, recv_sem, device)
        copy.start()
        sent.append(copy)

    for d in range(4):
        send(att_ref.at[(y + d) % NY], all_ref.at[me_global], send_sems.at[4 + d], recv_sems.at[4 + d], cross[d])
    here = remote(att_ref.at[y], all_ref.at[me_global], send_sems.at[0], recv_sems.at[0], near[0])
    local = pltpu.make_async_copy(att_ref.at[y], all_ref.at[me_global], recv_sems.at[0])

    @pl.when(stays)
    def _():
        local.start()

    @pl.when(jnp.logical_not(stays))
    def _():
        here.start()

    for d in range(1, 4):
        send(att_ref.at[(y + d) % NY], all_ref.at[me_global], send_sems.at[d], recv_sems.at[d], near[d])

    def of(source_hi, source_lo, d):
        return all_ref.at[(source_hi * 2 + source_lo) * 4 + (y + NY - d) % NY]

    for d in (0, 1, 3, 2):
        got = of(x_hi, core, d)
        if d == 0:
            @pl.when(stays)
            def _():
                local.wait()

            @pl.when(jnp.logical_not(stays))
            def _():
                here.wait_recv()
        else:
            remote(got, got, send_sems.at[d], recv_sems.at[d], near[d]).wait_recv()
        send(got, got, c_send.at[d], c_recv.at[d], twin)
    for d in (0, 1, 3, 2):
        got = of(1 - x_hi, core, d)
        remote(got, got, send_sems.at[4 + d], recv_sems.at[4 + d], cross[d]).wait_recv()
        send(got, got, c_send.at[4 + d], c_recv.at[4 + d], twin)
    for d in (0, 1, 3, 2):
        got = of(x_hi, 1 - core, d)
        remote(got, got, c_send.at[d], c_recv.at[d], twin).wait_recv()
    for d in (0, 1, 3, 2):
        got = of(1 - x_hi, 1 - core, d)
        remote(got, got, c_send.at[4 + d], c_recv.at[4 + d], twin).wait_recv()

    @pl.when(jnp.logical_not(stays))
    def _():
        here.wait_send()

    for copy in sent:
        copy.wait_send()


def give_back(attended):
    anywhere = pl.BlockSpec(memory_space=pl.ANY)
    dma = pltpu.SemaphoreType.DMA
    return pl.pallas_call(
        return_kernel,
        out_shape=jax.ShapeDtypeStruct((16, ROWS // 2, 128), BF16),
        in_specs=[anywhere],
        out_specs=anywhere,
        scratch_shapes=[dma((8,)), dma((8,)), dma((8,)), dma((8,))],
        compiler_params=pltpu.CompilerParams(collective_id=1, has_side_effects=True),
        name="give_back",
    )(attended)


def mix_kernel(att_ref, w_ref, out_ref):
    w = w_ref[...]
    half = ROWS // 2
    for side in range(2):
        cols = slice(side * HEAD_DIM, (side + 1) * HEAD_DIM)
        a = jnp.concatenate([att_ref[g][:, cols] for g in range(16)], axis=1)
        out_ref[side * half : (side + 1) * half, :] = jnp.dot(a, w, preferred_element_type=F32).astype(BF16)


def mix(attended, w_cols):
    whole = pl.BlockSpec(memory_space=pltpu.VMEM)
    return pl.pallas_call(
        mix_kernel,
        out_shape=jax.ShapeDtypeStruct((ROWS, 256), BF16),
        in_specs=[whole, whole],
        out_specs=whole,
        name="mix",
    )(attended, w_cols)


def body(tokens, w_query, w_key, w_value, w_out, block_mask, block_order):
    kv, query, lists = project(tokens, w_query, w_key, w_value, block_mask, block_order.reshape(1, NB))
    kv_all, q_all, w_all = exchange(kv, query, w_out)
    attended = attend(lists, q_all, kv_all.reshape(32 * ROWS, 128))
    everything = give_back(attended)
    return mix(everything, w_all.reshape(1024, 256))


def solution(mesh):
    placed = (P("ctx", None), P(None, "head"), P(None, "head"), P(None, "head"), P("head", None), P(), P())
    return jax.shard_map(body, mesh=mesh, in_specs=placed, out_specs=P("ctx", "head"), check_vma=False)
```

time: 652 us -> 82.7 us (0.13)
  waiting for transfers between devices: 304 us -> 0 us
  local copies, waits for them, and re-layouts: 223 us -> 4.54 us
  Pallas kernels: 0 us -> 77.8 us
  matrix products: 68.9 us -> 0 us
  other arithmetic: 37.6 us -> 0 us
  between operations: 13.5 us -> 0.04 us
    ppermute x31 -> x0, waiting for transfers between devices: 244 us -> none  [from_behind(): return lax.ppermute(value, axis, pairs)]
    gather x65 -> x0, local copies, waits for them, and re-layouts: 142 us -> none  [the longest x32 107 us: key_mask(): key_orig = jnp.take(block_order, key_blocks)]
    pallas_call x0 -> x5, Pallas kernels: none -> 77.8 us  [the longest x1 34.1 us: exchange(): pl.pallas_call(exchange_kernel, out_shape=(jax.ShapeDtypeStruct((32, ROWS...]
    dot_general x68 -> x0, matrix products: 68.9 us -> none  [the longest x32 35.7 us: attend(): jnp.einsum('hqk,khd->qhd', probs.astype(jnp.bfloat16), value_heads, prefe...]
    reduce_scatter x1 -> x0, waiting for transfers between devices: 59.6 us -> none  [body(): lax.psum_scatter(partial_out.astype(jnp.bfloat16), 'head', scatter_dimens...]
    broadcast_in_dim x32 -> x0, local copies, waits for them, and re-layouts: 51.1 us -> none  [key_mask(): return jnp.repeat(block_cols, BLOCK, axis=0) > 0]
    reduce_sum x32 -> x0, other arithmetic: 28.9 us -> none  [attend(): row_sum = row_sum * factor + jnp.sum(probs, axis=2)]
    while x93 -> x0, local copies, waits for them, and re-layouts: 28.7 us -> none
  transfers between devices with their start and end apart: 32 -> 0, of which waited for: 32 -> 0; matrix products, arithmetic and copies ran while one was open for 30% -> 0% of each run, Pallas kernels for 0% -> 0%
where the time goes in v1:
time: 82.7 us; the launch traced here: 82.4 us
  Pallas kernels  77.8 us (94%)
  local copies, waits for them, and re-layouts  4.54 us (5%)
    pallas_call x1, Pallas kernels, exchange(): pl.pallas_call(exchange_kernel, out_shape=(jax.ShapeDtypeStruct((32, ROWS...  34.1 us
    pallas_call x1, Pallas kernels, attend(): pl.pallas_call(attend_kernel, out_shape=jax.ShapeDtypeStruct((4, ROWS //...  23.3 us
    pallas_call x1, Pallas kernels, give_back(): pl.pallas_call(return_kernel, out_shape=jax.ShapeDtypeStruct((16, ROWS //...  13.9 us
    unnamed x8, local copies, waits for them, and re-layouts  4.54 us
    pallas_call x1, Pallas kernels, project(): pl.pallas_call(project_kernel, out_shape=(jax.ShapeDtypeStruct((4, ROWS,...  3.96 us
    pallas_call x1, Pallas kernels, mix(): pl.pallas_call(mix_kernel, out_shape=jax.ShapeDtypeStruct((ROWS, 256), BF...  2.54 us

profile of v1, /device:TPU:1, one launch (start us, length us, event | category | flops | bytes accessed | tf_op | source)
XLA Modules:
  0.0 82.4 jit_solution(14489845322473791634)
XLA Ops:
  0.0 4.0 %project.1 = (bf16[4,512,128]{2,1,0:T(8,128)(2,1)}, bf16[4,256,128]{2,1,0:T(8,128)(2,1)}, s32[32,128]{1,0:T(8,128)}) custom-call(bf16[512,1024]{1,0:T(8,128)(2,1)} %tok_ref.1, bf16[1024,256]{1,0:T(8,128)(2,1)} %wq_ref.1, bf16[1024,256]{1,0:T(8,128)(2,1)} %wk_ref.1, bf16[1024,256]{1,0:T(8,128)(2,1)} %wv_ref.1, s32[128,128]{1,0:T(8,128)} %mask_ref.1, ...), custom_call_target="tpu_custom_call" | custom-call | tf_op jit(solution)/shard_map/project/pallas_call | solution.py:71
  4.0 34.1 %exchange.1 = (bf16[32,512,128]{2,1,0:T(8,128)(2,1)}, bf16[4,256,128]{2,1,0:T(8,128)(2,1)}, bf16[4,256,256]{2,1,0:T(8,128)(2,1)}) custom-call(bf16[4,512,128]{2,1,0:T(8,128)(2,1)} %get-tuple-element.12.kv_ref, bf16[4,256,128]{2,1,0:T(8,128)(2,1)} %get-tuple-element.13.q_ref, bf16[256,1024]{1,0:T(8,128)(2,1)} %w_ref.1), custom_call_target="tpu_custom_call" | custom-call | tf_op jit(solution)/shard_map/exchange/pallas_call | solution.py:213
  38.0 0.0 copy-start
  38.1 2.2 %copy-done = bf16[32,512,128]{2,1,0:T(8,128)(2,1)S(1)} copy-done((bf16[32,512,128]{2,1,0:T(8,128)(2,1)S(1)}, bf16[32,512,128]{2,1,0:T(8,128)(2,1)}, u32[]{:S(2)}) %copy-start) | copy-done | bytes 4194328
  40.2 0.0 copy-start.2
  40.2 0.9 %copy-done.2 = bf16[4,256,128]{2,1,0:T(8,128)(2,1)S(1)} copy-done((bf16[4,256,128]{2,1,0:T(8,128)(2,1)S(1)}, bf16[4,256,128]{2,1,0:T(8,128)(2,1)}, u32[]{:S(2)}) %copy-start.2) | copy-done | bytes 262168
  41.2 0.0 copy-start.3
  41.2 0.7 copy-done.3
  41.9 23.3 %attend.1.att_ref = bf16[4,256,128]{2,1,0:T(8,128)(2,1)S(1)} custom-call(s32[32,128]{1,0:T(8,128)S(1)} %copy-done.3, bf16[4,256,128]{2,1,0:T(8,128)(2,1)S(1)} %copy-done.2, bf16[16384,128]{1,0:T(8,128)(2,1)S(1)} %bitcast.3), custom_call_target="tpu_custom_call" | custom-call | tf_op jit(solution)/shard_map/attend/pallas_call | solution.py:294
  65.2 0.0 copy-start.1
  65.2 0.7 copy-done.1
  65.9 13.9 %give_back.1.att_ref = bf16[16,256,128]{2,1,0:T(8,128)(2,1)} custom-call(bf16[4,256,128]{2,1,0:T(8,128)(2,1)} %copy-done.1), custom_call_target="tpu_custom_call" | custom-call | tf_op jit(solution)/shard_map/give_back/pallas_call | solution.py:394
  79.9 2.5 %mix.1 = bf16[512,256]{1,0:T(8,128)(2,1)} custom-call(bf16[16,256,128]{2,1,0:T(8,128)(2,1)} %give_back.1.att_ref, bf16[1024,256]{1,0:T(8,128)(2,1)} %bitcast.4), custom_call_target="tpu_custom_call" | custom-call | tf_op jit(solution)/shard_map/mix/pallas_call | solution.py:416
Async XLA Ops:
  38.0 2.2 %copy-start = (bf16[32,512,128]{2,1,0:T(8,128)(2,1)S(1)}, bf16[32,512,128]{2,1,0:T(8,128)(2,1)}, u32[]{:S(2)}) copy-start(bf16[32,512,128]{2,1,0:T(8,128)(2,1)} %get-tuple-element.15) | copy-start | bytes 12582916
  40.2 0.9 %copy-start.2 = (bf16[4,256,128]{2,1,0:T(8,128)(2,1)S(1)}, bf16[4,256,128]{2,1,0:T(8,128)(2,1)}, u32[]{:S(2)}) copy-start(bf16[4,256,128]{2,1,0:T(8,128)(2,1)} %get-tuple-element.14.q_ref) | copy-start | bytes 786436
  41.2 0.7 copy-start.3
  65.2 0.7 copy-start.1

commit v2 on v1

--- a/solution.py
+++ b/solution.py
@@ -28,61 +28,48 @@
     return (y * NZ + z) * 2 + x_lo
 
 
-def project_kernel(tok_ref, wq_ref, wk_ref, wv_ref, mask_ref, order_row_ref, kv_ref, q_ref, lists_ref):
-    tok = tok_ref[...]
-    keys = jnp.dot(tok, wk_ref[...], preferred_element_type=F32).astype(BF16)
-    vals = jnp.dot(tok, wv_ref[...], preferred_element_type=F32).astype(BF16)
-    query = jnp.dot(tok, wq_ref[...], preferred_element_type=F32).astype(BF16)
-    half = ROWS // 2
-    for j in range(4):
-        cols = slice(j * HEAD_DIM, (j + 1) * HEAD_DIM)
-        kv_ref[j] = jnp.concatenate([keys[:, cols], vals[:, cols]], axis=1)
-        q_ref[j] = jnp.concatenate([query[:half, cols], query[half:, cols]], axis=1)
-
-    _, z, _, _, core = place()
+def write_lists(mask, order_row, z, core, lists_ref):
     sub = lax.broadcasted_iota(jnp.int32, (NB, NB), 0)
     lane = lax.broadcasted_iota(jnp.int32, (NB, NB), 1)
-    initial_of = (order_row_ref[...] == sub).astype(F32).astype(BF16)
-    i16 = lax.broadcasted_iota(jnp.int32, (16, NB), 0)
-    l16 = lax.broadcasted_iota(jnp.int32, (16, NB), 1)
-    mine = ((i16 // 4 * NZ + z) * 2 + core) * 4 + i16 % 4
-    row_pick = (l16 == mine).astype(F32).astype(BF16)
-    rows_initial = lax.dot_general(
-        row_pick, initial_of, (((1,), (1,)), ((), ())), preferred_element_type=F32
-    ).astype(BF16)
-    mask = mask_ref[...].astype(F32).astype(BF16)
-    mask_rows = jnp.dot(rows_initial, mask, preferred_element_type=F32).astype(BF16)
+    nt = (((1,), (1,)), ((), ()))
+
+    def as_bf16(condition):
+        return condition.astype(F32).astype(BF16)
+
+    initial_of = as_bf16(order_row == sub)
+    mine = ((sub // 4 * NZ + z) * 2 + core) * 4 + sub % 4
+    row_pick = as_bf16(jnp.logical_and(lane == mine, sub < 16))
+    rows_initial = lax.dot_general(row_pick, initial_of, nt, preferred_element_type=F32).astype(BF16)
+    mask_rows = jnp.dot(rows_initial, mask.astype(F32).astype(BF16), preferred_element_type=F32).astype(BF16)
     allowed = jnp.dot(mask_rows, initial_of, preferred_element_type=F32)
-    before = (sub < lane).astype(F32).astype(BF16)
-    rank = jnp.dot(allowed.astype(BF16), before, preferred_element_type=F32)
+    rank = jnp.dot(allowed.astype(BF16), as_bf16(sub < lane), preferred_element_type=F32)
     rank = jnp.where(allowed > 0.5, rank, -1.0)
+    sub_f = sub.astype(F32)
     lane_row = lax.broadcasted_iota(jnp.int32, (8, NB), 1).astype(F32).astype(BF16)
-    sub_f = sub.astype(F32)
     for i in range(16):
-        hot = (rank[i : i + 1, :] == sub_f).astype(F32).astype(BF16)
-        got = lax.dot_general(lane_row, hot, (((1,), (1,)), ((), ())), preferred_element_type=F32)
+        hot = as_bf16(rank[i : i + 1, :] == sub_f)
+        got = lax.dot_general(lane_row, hot, nt, preferred_element_type=F32)
         lists_ref[i : i + 1, :] = got[0:1, :].astype(jnp.int32)
-    count = jnp.sum(allowed, axis=1, keepdims=True)
-    lists_ref[16:32, :] = jnp.broadcast_to(count, (16, NB)).astype(jnp.int32)
-
-
-def project(tokens, w_query, w_key, w_value, block_mask, order_row):
-    whole = pl.BlockSpec(memory_space=pltpu.VMEM)
-    return pl.pallas_call(
-        project_kernel,
-        out_shape=(
-            jax.ShapeDtypeStruct((4, ROWS, 128), BF16),
-            jax.ShapeDtypeStruct((4, ROWS // 2, 128), BF16),
-            jax.ShapeDtypeStruct((32, NB), jnp.int32),
-        ),
-        in_specs=[whole] * 6,
-        out_specs=(whole, whole, whole),
-        name="project",
-    )(tokens, w_query, w_key, w_value, block_mask, order_row)
-
-
-def exchange_kernel(kv_ref, q_ref, w_ref, kv_all, q_all, w_all, a_send, a_recv, q_send, q_recv, w_send, w_recv,
-                    z_send, z_recv, c_send, c_recv):
+    ones = jnp.ones((8, NB), BF16)
+    count = lax.dot_general(ones, allowed.astype(BF16), nt, preferred_element_type=F32)
+    steps = jnp.floor((count + 1.0) * 0.5)
+    total = jnp.sum(steps, axis=1, keepdims=True)
+    counts = jnp.where(lane[0:8] == 32, total, count).astype(jnp.int32)
+    lists_ref[16:32, :] = jnp.zeros((16, NB), jnp.int32)
+    lists_ref[17:18, :] = counts[0:1]
+
+
+def exchange_kernel(tok_hbm, wq_hbm, wk_hbm, wv_hbm, w_ref, mask_hbm, order_hbm, kv_all, q_all, w_all, lists_ref,
+                    tok_ref, wq_ref, wk_ref, wv_ref, mask_ref, order_ref, kv_ref, q_ref, in_sems,
+                    a_send, a_recv, q_send, q_recv, w_send, w_recv, z_send, z_recv, c_send, c_recv):
+    loads = [
+        pltpu.make_async_copy(src, dst, in_sems.at[n])
+        for n, (src, dst) in enumerate(
+            [(wk_hbm, wk_ref), (tok_hbm, tok_ref), (wv_hbm, wv_ref), (wq_hbm, wq_ref), (mask_hbm, mask_ref), (order_hbm, order_ref)]
+        )
+    ]
+    for load in loads:
+        load.start()
     y, z, x_lo, x_hi, core = place()
     me_ctx = ctx_of(y, z, x_lo)
     me_head = x_hi * 2 + core
@@ -102,6 +89,17 @@
     def _():
         pl.semaphore_signal(barrier, inc=1, device_id=a_to[0], device_id_type=MESH)
 
+    half = ROWS // 2
+    columns = [slice(j * HEAD_DIM, (j + 1) * HEAD_DIM) for j in range(4)]
+    loads[0].wait()
+    loads[1].wait()
+    tok = tok_ref[...]
+    keys = jnp.dot(tok, wk_ref[...], preferred_element_type=F32).astype(BF16)
+    loads[2].wait()
+    vals = jnp.dot(tok, wv_ref[...], preferred_element_type=F32).astype(BF16)
+    for j in range(4):
+        kv_ref[j] = jnp.concatenate([keys[:, columns[j]], vals[:, columns[j]]], axis=1)
+
     pl.semaphore_wait(barrier, 8 + (x_lo + core) % 2)
 
     def remote(src, dst, send_sem, recv_sem, device):
@@ -128,16 +126,27 @@
     @pl.when(stays)
     def _():
         kv_local.start()
-        q_local.start()
 
     @pl.when(jnp.logical_not(stays))
     def _():
         kv_here.start()
-        q_here.start()
 
     order = (1, 3, 2)
     for d in order:
         send(kv_ref.at[(y + d) % NY], kv_all.at[me_ctx], a_send.at[d], a_recv.at[d], a_to[d])
+    loads[3].wait()
+    query = jnp.dot(tok, wq_ref[...], preferred_element_type=F32).astype(BF16)
+    for j in range(4):
+        q_ref[j] = jnp.concatenate([query[:half, columns[j]], query[half:, columns[j]]], axis=1)
+
+    @pl.when(stays)
+    def _():
+        q_local.start()
+
+    @pl.when(jnp.logical_not(stays))
+    def _():
+        q_here.start()
+
     for d in order:
         send(q_ref.at[(y + d) % NY], q_all.at[y], q_send.at[d], q_recv.at[d], a_to[d])
     for k in range(1, 4):
@@ -166,6 +175,10 @@
         send(chunk(d, 0), chunk(d, 0), z_send.at[d], z_recv.at[d], up)
         send(chunk(d, 0), chunk(d, 0), z_send.at[4 + d], z_recv.at[4 + d], down)
         send(chunk(d, 0), chunk(d, 0), c_send.at[d], c_recv.at[d], twin)
+        if d == 0:
+            loads[4].wait()
+            loads[5].wait()
+            write_lists(mask_ref[...], order_ref[...], z, core, lists_ref)
     for d in (0, 1, 3, 2):
         below, above = chunk(d, -1), chunk(d, 1)
         arrived(below, z_send.at[d], z_recv.at[d], up)
@@ -207,90 +220,140 @@
         copy.wait_send()
 
 
-def exchange(kv, query, w_out):
+def exchange(tokens, w_query, w_key, w_value, w_out, block_mask, order_row):
+    in_hbm = pl.BlockSpec(memory_space=pltpu.HBM)
+    operands = [tokens, w_query, w_key, w_value, w_out, block_mask, order_row]
+    operands = [pltpu.with_memory_space_constraint(a, pltpu.HBM) for a in operands]
     anywhere = pl.BlockSpec(memory_space=pl.ANY)
     dma = pltpu.SemaphoreType.DMA
+    vmem = pltpu.VMEM
     return pl.pallas_call(
         exchange_kernel,
         out_shape=(
             jax.ShapeDtypeStruct((32, ROWS, 128), BF16),
             jax.ShapeDtypeStruct((4, ROWS // 2, 128), BF16),
             jax.ShapeDtypeStruct((4, 256, 256), BF16),
+            jax.ShapeDtypeStruct((32, NB), jnp.int32),
         ),
-        in_specs=[anywhere] * 3,
-        out_specs=(anywhere,) * 3,
+        in_specs=[in_hbm] * 7,
+        out_specs=(anywhere,) * 3 + (pl.BlockSpec(memory_space=vmem),),
         scratch_shapes=[
+            vmem((ROWS, 1024), BF16), vmem((1024, 256), BF16), vmem((1024, 256), BF16), vmem((1024, 256), BF16),
+            vmem((NB, NB), jnp.int32), vmem((1, NB), jnp.int32), vmem((4, ROWS, 128), BF16), vmem((4, ROWS // 2, 128), BF16),
+            dma((6,)),
             dma((4,)), dma((4,)), dma((4,)), dma((4,)), dma((4,)), dma((4,)),
             dma((12,)), dma((12,)), dma((16,)), dma((16,)),
         ],
-        compiler_params=pltpu.CompilerParams(collective_id=0, has_side_effects=True),
+        compiler_params=pltpu.CompilerParams(collective_id=0, has_side_effects=True, vmem_limit_bytes=16 << 20),
         name="exchange",
-    )(kv, query, w_out)
+    )(*operands)
 
 
 UNROLL = 4
 EXP2_SCALE = (HEAD_DIM ** -0.5) * 1.4426950408889634
-
-
-def attend_kernel(lists, q_ref, kv_ref, out_ref, qz, scores):
-    lanes = lax.broadcasted_iota(jnp.int32, (BLOCK, 128), 1)
-    nt = (((1,), (1,)), ((), ()))
-
-    def owner(step, _):
-        for b in range(4):
-            row0 = (b % 2) * BLOCK
-            q = q_ref[step, row0 : row0 + BLOCK, :]
-            if b // 2:
-                q = jnp.concatenate([q[:, HEAD_DIM:], q[:, :HEAD_DIM]], axis=1)
-            qz[b] = jnp.where(lanes < HEAD_DIM, q, jnp.zeros_like(q))
-        for b in range(4):
-            i = step * 4 + b
-            n = lists[16 + i, 0]
-            groups = (n + UNROLL - 1) // UNROLL
-            q = qz[b]
-
-            def keys_at(k):
-                start = pl.multiple_of(lists[i, k] * BLOCK, BLOCK)
-                return kv_ref[pl.ds(start, BLOCK), :]
-
-            def first(g, top):
-                for u in range(UNROLL):
-                    k = g * UNROLL + u
-                    bias = jnp.where(k < n, 0.0, LIST_PAD).astype(F32)
-                    s = lax.dot_general(q, keys_at(k), nt, preferred_element_type=F32) + bias
-                    scores[k] = s
-                    top = jnp.maximum(top, s)
-                return top
-
-            top = lax.fori_loop(0, groups, first, jnp.full((BLOCK, BLOCK), -3e38, F32))
+SMALLEST, LARGEST = 1e-20, 1e30
+NT = (((1,), (1,)), ((), ()))
+
+
+def query_place(i):
+    b = i % 4
+    return i // 4, slice(b % 2 * BLOCK, (b % 2 + 1) * BLOCK), slice(b // 2 * HEAD_DIM, (b // 2 + 1) * HEAD_DIM)
+
+
+def attend_kernel(lists, q_ref, kv_ref, out_ref, qz, acc, ones_v, sbuf, scores):
+    left = lax.broadcasted_iota(jnp.int32, (BLOCK, 128), 1) < HEAD_DIM
+    zero = jnp.zeros((BLOCK, 128), F32)
+    for i in range(16):
+        y, rows, cols = query_place(i)
+        q = q_ref[y, rows, :]
+        if cols.start:
+            q = jnp.concatenate([q[:, HEAD_DIM:], q[:, :HEAD_DIM]], axis=1)
+        qz[i] = jnp.where(left, q, jnp.zeros_like(q))
+        acc[i] = zero
+    qz[16] = jnp.zeros((BLOCK, 128), BF16)
+    acc[16] = zero
+
+    def fill(t, _):
+        part = pl.ds(pl.multiple_of(t * 1024, 1024), 1024)
+        lanes = lax.broadcasted_iota(jnp.int32, (1024, 128), 1)
+        ones_v[part, :] = jnp.where(lanes < HEAD_DIM, jnp.ones((1024, 128), BF16), kv_ref[part, :])
+        return 0
+
+    lax.fori_loop(0, 16, fill, 0)
+    second = lax.broadcasted_iota(jnp.int32, (1, 2 * BLOCK), 1) >= BLOCK
+
+    def rows_at(i, k):
+        return pl.ds(pl.multiple_of(lists[i, jnp.minimum(k, NB - 1)] * BLOCK, BLOCK), BLOCK)
+
+    def advance(i, k):
+        done = k + 2 >= lists[17, i]
+        return jnp.minimum(jnp.where(done, i + 1, i), 16), jnp.where(done, 0, k + 2)
+
+    def score(slot, i, k):
+        for u in range(UNROLL):
+            keys = jnp.concatenate([kv_ref[rows_at(i, k), :], kv_ref[rows_at(i, k + 1), :]], axis=0)
+            sbuf[slot, u] = lax.dot_general(qz[i], keys, NT, preferred_element_type=F32)
+            i, k = advance(i, k)
+        return i, k
+
+    def weigh(slot, i, k):
+        for u in range(UNROLL):
+            bias = jnp.where(k + 1 < lists[17, i], 0.0, LIST_PAD).astype(F32)
+            vals = jnp.concatenate([ones_v[rows_at(i, k), :], ones_v[rows_at(i, k + 1), :]], axis=0)
+            p = jnp.exp2(sbuf[slot, u] * EXP2_SCALE + jnp.where(second, bias, 0.0)).astype(BF16)
+            acc[i] += jnp.dot(p, vals, preferred_element_type=F32)
+            i, k = advance(i, k)
+
+    start = jnp.int32(0)
+    i1, k1 = score(0, start, start)
+
+    def step(_, carry):
+        i, k, i1, k1 = carry
+        i2, k2 = score(1, i1, k1)
+        weigh(0, i, k)
+        i3, k3 = score(0, i2, k2)
+        weigh(1, i1, k1)
+        return i2, k2, i3, k3
+
+    lax.fori_loop(0, (lists[17, 32] + 2 * UNROLL - 1) // (2 * UNROLL), step, (start, start, i1, k1))
+
+    fine = jnp.full((BLOCK, HEAD_DIM), 1.0, F32)
+    for i in range(16):
+        y, rows, cols = query_place(i)
+        denom = acc[i][:, :HEAD_DIM]
+        within = jnp.logical_and(denom >= SMALLEST, denom <= LARGEST)
+        fine = jnp.where(within, fine, 0.0)
+        out_ref[y, rows, cols] = (acc[i][:, HEAD_DIM:] / denom).astype(BF16)
+
+    @pl.when(jnp.min(fine) < 0.5)
+    def _():
+        for i in range(16):
+            y, rows, cols = query_place(i)
+            n = lists[17, i]
+
+            def first(k, top):
+                s = lax.dot_general(qz[i], kv_ref[rows_at(i, k), :], NT, preferred_element_type=F32)
+                scores[k] = s
+                return jnp.maximum(top, s)
+
+            top = lax.fori_loop(0, n, first, jnp.full((BLOCK, BLOCK), -3e38, F32))
             top = jnp.max(top, axis=1, keepdims=True)
 
-            def second(g, carry):
-                total, acc = carry
-                probs, blocks = [], []
-                for u in range(UNROLL):
-                    k = g * UNROLL + u
-                    p = jnp.exp2((scores[k] - top) * EXP2_SCALE)
-                    total = total + p
-                    probs.append(p.astype(BF16))
-                    blocks.append(keys_at(k))
-                acc = acc + jnp.dot(
-                    jnp.concatenate(probs, axis=1), jnp.concatenate(blocks, axis=0), preferred_element_type=F32
+            def then(k, carry):
+                total, weighted = carry
+                p = jnp.exp2((scores[k] - top) * EXP2_SCALE)
+                return total + p, weighted + jnp.dot(
+                    p.astype(BF16), kv_ref[rows_at(i, k), :], preferred_element_type=F32
                 )
-                return total, acc
-
-            zero = jnp.zeros((BLOCK, 128), F32)
-            total, acc = lax.fori_loop(0, groups, second, (zero, zero))
+
+            total, weighted = lax.fori_loop(0, n, then, (zero, zero))
             denom = jnp.sum(total, axis=1, keepdims=True)
-            row0, col0 = (b % 2) * BLOCK, (b // 2) * HEAD_DIM
-            out_ref[step, row0 : row0 + BLOCK, col0 : col0 + HEAD_DIM] = (acc[:, HEAD_DIM:] / denom).astype(BF16)
-        return 0
-
-    lax.fori_loop(0, 4, owner, 0)
+            out_ref[y, rows, cols] = (weighted[:, HEAD_DIM:] / denom).astype(BF16)
 
 
 def attend(lists, query, kv):
     whole = pl.BlockSpec(memory_space=pltpu.VMEM)
+    vmem = pltpu.VMEM
     return pl.pallas_call(
         attend_kernel,
         out_shape=jax.ShapeDtypeStruct((4, ROWS // 2, 128), BF16),
@@ -299,9 +362,15 @@
             grid=(),
             in_specs=[whole, whole],
             out_specs=whole,
-            scratch_shapes=[pltpu.VMEM((4, BLOCK, 128), BF16), pltpu.VMEM((NB, BLOCK, BLOCK), F32)],
+            scratch_shapes=[
+                vmem((17, BLOCK, 128), BF16),
+                vmem((17, BLOCK, 128), F32),
+                vmem((32 * ROWS, 128), BF16),
+                vmem((2, UNROLL, BLOCK, 2 * BLOCK), F32),
+                vmem((NB, BLOCK, BLOCK), F32),
+            ],
         ),
-        compiler_params=pltpu.CompilerParams(vmem_limit_bytes=32 << 20),
+        compiler_params=pltpu.CompilerParams(vmem_limit_bytes=28 << 20),
         name="attend",
     )(lists, query, kv)
 
@@ -397,7 +466,7 @@
         in_specs=[anywhere],
         out_specs=anywhere,
         scratch_shapes=[dma((8,)), dma((8,)), dma((8,)), dma((8,))],
-        compiler_params=pltpu.CompilerParams(collective_id=1, has_side_effects=True),
+        compiler_params=pltpu.CompilerParams(collective_id=1, has_side_effects=True, vmem_limit_bytes=16 << 20),
         name="give_back",
     )(attended)
 
@@ -418,13 +487,15 @@
         out_shape=jax.ShapeDtypeStruct((ROWS, 256), BF16),
         in_specs=[whole, whole],
         out_specs=whole,
+        compiler_params=pltpu.CompilerParams(vmem_limit_bytes=16 << 20),
         name="mix",
     )(attended, w_cols)
 
 
 def body(tokens, w_query, w_key, w_value, w_out, block_mask, block_order):
-    kv, query, lists = project(tokens, w_query, w_key, w_value, block_mask, block_order.reshape(1, NB))
-    kv_all, q_all, w_all = exchange(kv, query, w_out)
+    kv_all, q_all, w_all, lists = exchange(
+        tokens, w_query, w_key, w_value, w_out, block_mask, block_order.reshape(1, NB)
+    )
     attended = attend(lists, q_all, kv_all.reshape(32 * ROWS, 128))
     everything = give_back(attended)
     return mix(everything, w_all.reshape(1024, 256))

time: 82.7 us -> 103 us (1.25)
  Pallas kernels: 77.8 us -> 103 us
  local copies, waits for them, and re-layouts: 4.54 us -> 0 us
    pallas_call x1, Pallas kernels: 23.3 us -> 56.4 us  [attend(): pl.pallas_call(attend_kernel, out_shape=jax.ShapeDtypeStruct((4, ROWS //...]
    unnamed x8 -> x0, local copies, waits for them, and re-layouts: 4.54 us -> none
    pallas_call x1 -> x0, Pallas kernels: 3.96 us -> none  [project(): pl.pallas_call(project_kernel, out_shape=(jax.ShapeDtypeStruct((4, ROWS,...]
    pallas_call x1, Pallas kernels: 34.1 us -> 31.7 us  [exchange(): pl.pallas_call(exchange_kernel, out_shape=(jax.ShapeDtypeStruct((32, ROWS...]
    pallas_call x1, Pallas kernels: 2.54 us -> 1.19 us  [mix(): pl.pallas_call(mix_kernel, out_shape=jax.ShapeDtypeStruct((ROWS, 256), BF...]
where the time goes in v2:
time: 103 us
  Pallas kernels  103 us (100%)
    pallas_call x1, Pallas kernels, attend(): pl.pallas_call(attend_kernel, out_shape=jax.ShapeDtypeStruct((4, ROWS //...  56.4 us
    pallas_call x1, Pallas kernels, exchange(): pl.pallas_call(exchange_kernel, out_shape=(jax.ShapeDtypeStruct((32, ROWS...  31.7 us
    pallas_call x1, Pallas kernels, give_back(): pl.pallas_call(return_kernel, out_shape=jax.ShapeDtypeStruct((16, ROWS //...  13.5 us

profile of v2, /device:TPU:1, one launch (start us, length us, event | category | flops | bytes accessed | tf_op | source)
XLA Modules:
  0.0 102.8 jit_solution(12453186010345533533)
XLA Ops:
  0.0 31.7 %exchange.1 = (bf16[32,512,128]{2,1,0:T(8,128)(2,1)S(1)}, bf16[4,256,128]{2,1,0:T(8,128)(2,1)S(1)}, bf16[4,256,256]{2,1,0:T(8,128)(2,1)S(1)}, s32[32,128]{1,0:T(8,128)S(1)}) custom-call(bf16[512,1024]{1,0:T(8,128)(2,1)} %tok_hbm.1, bf16[1024,256]{1,0:T(8,128)(2,1)} %wq_hbm.1, bf16[1024,256]{1,0:T(8,128)(2,1)} %wk_hbm.1, bf16[1024,256]{1,0:T(8,128)(2,1)} %wv_hbm.1, ...), custom_call_target="tpu_custom_call" | custom-call | tf_op jit(solution)/shard_map/exchange/pallas_call | solution.py:230
  31.7 56.4 %attend.1.att_ref = bf16[4,256,128]{2,1,0:T(8,128)(2,1)S(1)} custom-call(s32[32,128]{1,0:T(8,128)S(1)} %get-tuple-element.9.lists, bf16[4,256,128]{2,1,0:T(8,128)(2,1)S(1)} %get-tuple-element.10.q_ref, bf16[16384,128]{1,0:T(8,128)(2,1)S(1)} %bitcast.3), custom_call_target="tpu_custom_call" | custom-call | tf_op jit(solution)/shard_map/attend/pallas_call | solution.py:357
  88.1 13.5 %give_back.1.att_ref = bf16[16,256,128]{2,1,0:T(8,128)(2,1)S(1)} custom-call(bf16[4,256,128]{2,1,0:T(8,128)(2,1)S(1)} %attend.1.att_ref), custom_call_target="tpu_custom_call" | custom-call | tf_op jit(solution)/shard_map/give_back/pallas_call | solution.py:463
  101.6 1.2 %mix.1 = bf16[512,256]{1,0:T(8,128)(2,1)} custom-call(bf16[16,256,128]{2,1,0:T(8,128)(2,1)S(1)} %give_back.1.att_ref, bf16[1024,256]{1,0:T(8,128)(2,1)S(1)} %bitcast.4), custom_call_target="tpu_custom_call" | custom-call | tf_op jit(solution)/shard_map/mix/pallas_call | solution.py:485

commit v3 on v2

--- a/solution.py
+++ b/solution.py
@@ -59,8 +59,14 @@
     lists_ref[17:18, :] = counts[0:1]
 
 
-def exchange_kernel(tok_hbm, wq_hbm, wk_hbm, wv_hbm, w_ref, mask_hbm, order_hbm, kv_all, q_all, w_all, lists_ref,
-                    tok_ref, wq_ref, wk_ref, wv_ref, mask_ref, order_ref, kv_ref, q_ref, in_sems,
+def query_place(i):
+    b = i % 4
+    return i // 4, slice(b % 2 * BLOCK, (b % 2 + 1) * BLOCK), slice(b // 2 * HEAD_DIM, (b // 2 + 1) * HEAD_DIM)
+
+
+def exchange_kernel(tok_hbm, wq_hbm, wk_hbm, wv_hbm, w_ref, mask_hbm, order_hbm,
+                    kv_all, ones_v, w_all, lists_ref, qz,
+                    tok_ref, wq_ref, wk_ref, wv_ref, mask_ref, order_ref, kv_ref, q_ref, q_all, in_sems,
                     a_send, a_recv, q_send, q_recv, w_send, w_recv, z_send, z_recv, c_send, c_recv):
     loads = [
         pltpu.make_async_copy(src, dst, in_sems.at[n])
@@ -131,55 +137,21 @@
     def _():
         kv_here.start()
 
-    order = (1, 3, 2)
-    for d in order:
+    def send_kv(d):
         send(kv_ref.at[(y + d) % NY], kv_all.at[me_ctx], a_send.at[d], a_recv.at[d], a_to[d])
-    loads[3].wait()
-    query = jnp.dot(tok, wq_ref[...], preferred_element_type=F32).astype(BF16)
-    for j in range(4):
-        q_ref[j] = jnp.concatenate([query[:half, columns[j]], query[half:, columns[j]]], axis=1)
-
-    @pl.when(stays)
-    def _():
-        q_local.start()
-
-    @pl.when(jnp.logical_not(stays))
-    def _():
-        q_here.start()
-
-    for d in order:
+
+    def send_q(d):
         send(q_ref.at[(y + d) % NY], q_all.at[y], q_send.at[d], q_recv.at[d], a_to[d])
-    for k in range(1, 4):
-        to = (me_head + k) % 4
-        send(w_ref.at[:, pl.ds(pl.multiple_of(to * 256, 256), 256)], w_all.at[me_head], w_send.at[k - 1], w_recv.at[k - 1],
-             head_peers[k - 1])
-    w_local = pltpu.make_async_copy(
-        w_ref.at[:, pl.ds(pl.multiple_of(me_head * 256, 256), 256)], w_all.at[me_head], w_recv.at[3]
-    )
-    w_local.start()
 
     def chunk(d, dz):
         return kv_all.at[ctx_of((y + NY - d) % NY, (z + NZ + dz) % NZ, core)]
 
-    for d in (0, 1, 3, 2):
-        if d == 0:
-            @pl.when(stays)
-            def _():
-                kv_local.wait()
-
-            @pl.when(jnp.logical_not(stays))
-            def _():
-                kv_here.wait_recv()
-        else:
-            arrived(chunk(d, 0), a_send.at[d], a_recv.at[d], a_to[d])
+    def pass_on(d):
         send(chunk(d, 0), chunk(d, 0), z_send.at[d], z_recv.at[d], up)
         send(chunk(d, 0), chunk(d, 0), z_send.at[4 + d], z_recv.at[4 + d], down)
         send(chunk(d, 0), chunk(d, 0), c_send.at[d], c_recv.at[d], twin)
-        if d == 0:
-            loads[4].wait()
-            loads[5].wait()
-            write_lists(mask_ref[...], order_ref[...], z, core, lists_ref)
-    for d in (0, 1, 3, 2):
+
+    def from_near(d):
         below, above = chunk(d, -1), chunk(d, 1)
         arrived(below, z_send.at[d], z_recv.at[d], up)
         if d in (0, 1):
@@ -189,30 +161,111 @@
         if d in (2, 3):
             send(above, above, z_send.at[8 + d], z_recv.at[8 + d], down)
         send(above, above, c_send.at[8 + d], c_recv.at[8 + d], twin)
+
+    order = (1, 3, 2)
+    send_kv(1)
+    send_kv(3)
+    send_kv(2)
+
+    @pl.when(stays)
+    def _():
+        kv_local.wait()
+
+    @pl.when(jnp.logical_not(stays))
+    def _():
+        kv_here.wait_recv()
+
+    pass_on(0)
+    loads[3].wait()
+    query = jnp.dot(tok, wq_ref[...], preferred_element_type=F32).astype(BF16)
+    for j in range(4):
+        q_ref[j] = jnp.concatenate([query[:half, columns[j]], query[half:, columns[j]]], axis=1)
+
+    @pl.when(stays)
+    def _():
+        q_local.start()
+
+    @pl.when(jnp.logical_not(stays))
+    def _():
+        q_here.start()
+
+    for d in order:
+        send_q(d)
+    arrived(chunk(1, 0), a_send.at[1], a_recv.at[1], a_to[1])
+    pass_on(1)
+    arrived(chunk(3, 0), a_send.at[3], a_recv.at[3], a_to[3])
+    pass_on(3)
+    arrived(chunk(2, 0), a_send.at[2], a_recv.at[2], a_to[2])
+    pass_on(2)
+    from_near(0)
+    for k in range(1, 4):
+        to = (me_head + k) % 4
+        send(w_ref.at[:, pl.ds(pl.multiple_of(to * 256, 256), 256)], w_all.at[me_head], w_send.at[k - 1], w_recv.at[k - 1],
+             head_peers[k - 1])
+    w_local = pltpu.make_async_copy(
+        w_ref.at[:, pl.ds(pl.multiple_of(me_head * 256, 256), 256)], w_all.at[me_head], w_recv.at[3]
+    )
+    w_local.start()
+    from_near(1)
+    loads[4].wait()
+    loads[5].wait()
+    write_lists(mask_ref[...], order_ref[...], z, core, lists_ref)
+
+    def twin_arrived(d, dz, place_of):
+        got = kv_all.at[ctx_of((y + NY - d) % NY, (z + NZ + dz) % NZ, 1 - core)]
+        arrived(got, c_send.at[place_of + d], c_recv.at[place_of + d], twin)
+
+    left = lax.broadcasted_iota(jnp.int32, (ROWS, 128), 1) < HEAD_DIM
+
+    def lay_out(d, dz, sides=(0, 1)):
+        for side in sides:
+            ctx = ctx_of((y + NY - d) % NY, (z + NZ + dz) % NZ, side)
+            rows = pl.ds(pl.multiple_of(ctx * ROWS, ROWS), ROWS)
+            got = kv_all[ctx]
+            ones_v[rows, :] = jnp.where(left, jnp.ones_like(got), got)
+
+    @pl.when(stays)
+    def _():
+        q_local.wait()
+
+    @pl.when(jnp.logical_not(stays))
+    def _():
+        q_here.wait_recv()
+
+    for d in order:
+        arrived(q_all.at[(y + NY - d) % NY], q_send.at[d], q_recv.at[d], a_to[d])
+    narrow = lax.broadcasted_iota(jnp.int32, (BLOCK, 128), 1) < HEAD_DIM
+    for i in range(16):
+        step, rows, cols = query_place(i)
+        q = q_all[step, rows, :]
+        if cols.start:
+            q = jnp.concatenate([q[:, HEAD_DIM:], q[:, :HEAD_DIM]], axis=1)
+        qz[i] = jnp.where(narrow, q, jnp.zeros_like(q))
+    qz[16] = jnp.zeros((BLOCK, 128), BF16)
+    for d in (0, 1, 3, 2):
+        twin_arrived(d, 0, 0)
+        lay_out(d, 0)
+    from_near(3)
+    from_near(2)
+    for d in (0, 1, 3, 2):
+        twin_arrived(d, -1, 4)
+        twin_arrived(d, 1, 8)
+        lay_out(d, -1)
+        lay_out(d, 1)
     for d in (0, 1, 3, 2):
         far = chunk(d, 2)
         arrived(far, z_send.at[8 + d], z_recv.at[8 + d], up)
         send(far, far, c_send.at[12 + d], c_recv.at[12 + d], twin)
-
-    def twin_chunk(d, dz):
-        return kv_all.at[ctx_of((y + NY - d) % NY, (z + NZ + dz) % NZ, 1 - core)]
-
-    for place_of, dz in ((0, 0), (4, -1), (8, 1), (12, 2)):
-        for d in (0, 1, 3, 2):
-            arrived(twin_chunk(d, dz), c_send.at[place_of + d], c_recv.at[place_of + d], twin)
-
-    @pl.when(stays)
-    def _():
-        q_local.wait()
-
-    @pl.when(jnp.logical_not(stays))
-    def _():
-        q_here.wait_recv()
+        lay_out(d, 2, (core,))
+    for d in (0, 1, 3, 2):
+        twin_arrived(d, 2, 12)
+        lay_out(d, 2, (1 - core,))
+
+    @pl.when(jnp.logical_not(stays))
+    def _():
         kv_here.wait_send()
         q_here.wait_send()
 
-    for d in order:
-        arrived(q_all.at[(y + NY - d) % NY], q_send.at[d], q_recv.at[d], a_to[d])
     for k in range(1, 4):
         arrived(w_all.at[(me_head + 4 - k) % 4], w_send.at[k - 1], w_recv.at[k - 1], head_peers[k - 1])
     w_local.wait()
@@ -227,59 +280,40 @@
     anywhere = pl.BlockSpec(memory_space=pl.ANY)
     dma = pltpu.SemaphoreType.DMA
     vmem = pltpu.VMEM
+    in_vmem = pl.BlockSpec(memory_space=vmem)
     return pl.pallas_call(
         exchange_kernel,
         out_shape=(
             jax.ShapeDtypeStruct((32, ROWS, 128), BF16),
-            jax.ShapeDtypeStruct((4, ROWS // 2, 128), BF16),
+            jax.ShapeDtypeStruct((32 * ROWS, 128), BF16),
             jax.ShapeDtypeStruct((4, 256, 256), BF16),
             jax.ShapeDtypeStruct((32, NB), jnp.int32),
+            jax.ShapeDtypeStruct((17, BLOCK, 128), BF16),
         ),
         in_specs=[in_hbm] * 7,
-        out_specs=(anywhere,) * 3 + (pl.BlockSpec(memory_space=vmem),),
+        out_specs=(in_vmem, in_vmem, anywhere, in_vmem, in_vmem),
         scratch_shapes=[
             vmem((ROWS, 1024), BF16), vmem((1024, 256), BF16), vmem((1024, 256), BF16), vmem((1024, 256), BF16),
             vmem((NB, NB), jnp.int32), vmem((1, NB), jnp.int32), vmem((4, ROWS, 128), BF16), vmem((4, ROWS // 2, 128), BF16),
-            dma((6,)),
+            vmem((4, ROWS // 2, 128), BF16), dma((6,)),
             dma((4,)), dma((4,)), dma((4,)), dma((4,)), dma((4,)), dma((4,)),
             dma((12,)), dma((12,)), dma((16,)), dma((16,)),
         ],
-        compiler_params=pltpu.CompilerParams(collective_id=0, has_side_effects=True, vmem_limit_bytes=16 << 20),
+        compiler_params=pltpu.CompilerParams(collective_id=0, has_side_effects=True, vmem_limit_bytes=24 << 20),
         name="exchange",
     )(*operands)
 
 
-UNROLL = 4
+UNROLL = 8
 EXP2_SCALE = (HEAD_DIM ** -0.5) * 1.4426950408889634
 SMALLEST, LARGEST = 1e-20, 1e30
 NT = (((1,), (1,)), ((), ()))
 
 
-def query_place(i):
-    b = i % 4
-    return i // 4, slice(b % 2 * BLOCK, (b % 2 + 1) * BLOCK), slice(b // 2 * HEAD_DIM, (b // 2 + 1) * HEAD_DIM)
-
-
-def attend_kernel(lists, q_ref, kv_ref, out_ref, qz, acc, ones_v, sbuf, scores):
-    left = lax.broadcasted_iota(jnp.int32, (BLOCK, 128), 1) < HEAD_DIM
+def attend_kernel(lists, kv_ref, ones_v, qz, out_ref, acc, sbuf, scores):
     zero = jnp.zeros((BLOCK, 128), F32)
-    for i in range(16):
-        y, rows, cols = query_place(i)
-        q = q_ref[y, rows, :]
-        if cols.start:
-            q = jnp.concatenate([q[:, HEAD_DIM:], q[:, :HEAD_DIM]], axis=1)
-        qz[i] = jnp.where(left, q, jnp.zeros_like(q))
+    for i in range(17):
         acc[i] = zero
-    qz[16] = jnp.zeros((BLOCK, 128), BF16)
-    acc[16] = zero
-
-    def fill(t, _):
-        part = pl.ds(pl.multiple_of(t * 1024, 1024), 1024)
-        lanes = lax.broadcasted_iota(jnp.int32, (1024, 128), 1)
-        ones_v[part, :] = jnp.where(lanes < HEAD_DIM, jnp.ones((1024, 128), BF16), kv_ref[part, :])
-        return 0
-
-    lax.fori_loop(0, 16, fill, 0)
     second = lax.broadcasted_iota(jnp.int32, (1, 2 * BLOCK), 1) >= BLOCK
 
     def rows_at(i, k):
@@ -351,7 +385,7 @@
             out_ref[y, rows, cols] = (weighted[:, HEAD_DIM:] / denom).astype(BF16)
 
 
-def attend(lists, query, kv):
+def attend(lists, kv, ones_v, qz):
     whole = pl.BlockSpec(memory_space=pltpu.VMEM)
     vmem = pltpu.VMEM
     return pl.pallas_call(
@@ -360,19 +394,17 @@
         grid_spec=pltpu.PrefetchScalarGridSpec(
             num_scalar_prefetch=1,
             grid=(),
-            in_specs=[whole, whole],
+            in_specs=[whole] * 3,
             out_specs=whole,
             scratch_shapes=[
-                vmem((17, BLOCK, 128), BF16),
                 vmem((17, BLOCK, 128), F32),
-                vmem((32 * ROWS, 128), BF16),
                 vmem((2, UNROLL, BLOCK, 2 * BLOCK), F32),
                 vmem((NB, BLOCK, BLOCK), F32),
             ],
         ),
-        compiler_params=pltpu.CompilerParams(vmem_limit_bytes=28 << 20),
+        compiler_params=pltpu.CompilerParams(vmem_limit_bytes=24 << 20),
         name="attend",
-    )(lists, query, kv)
+    )(lists, kv, ones_v, qz)
 
 
 def return_kernel(att_ref, all_ref, send_sems, recv_sems, c_send, c_recv):
@@ -493,10 +525,10 @@
 
 
 def body(tokens, w_query, w_key, w_value, w_out, block_mask, block_order):
-    kv_all, q_all, w_all, lists = exchange(
+    kv, ones_v, w_all, lists, qz = exchange(
         tokens, w_query, w_key, w_value, w_out, block_mask, block_order.reshape(1, NB)
     )
-    attended = attend(lists, q_all, kv_all.reshape(32 * ROWS, 128))
+    attended = attend(lists, kv.reshape(32 * ROWS, 128), ones_v, qz)
     everything = give_back(attended)
     return mix(everything, w_all.reshape(1024, 256))
 

time: 103 us -> 105 us (1.019)
  the two profiles are of different devices: /device:TPU:1 before, /device:TPU:97 now
where the time goes in v3:
time: 105 us
  Pallas kernels  105 us (100%)
    pallas_call x1, Pallas kernels, attend(): pl.pallas_call(attend_kernel, out_shape=jax.ShapeDtypeStruct((4, ROWS //...  42.7 us
    pallas_call x1, Pallas kernels, give_back(): pl.pallas_call(return_kernel, out_shape=jax.ShapeDtypeStruct((16, ROWS //...  32.9 us
    pallas_call x1, Pallas kernels, exchange(): pl.pallas_call(exchange_kernel, out_shape=(jax.ShapeDtypeStruct((32, ROWS...  28.3 us

profile of v3, /device:TPU:97, one launch (start us, length us, event | category | flops | bytes accessed | tf_op | source)
XLA Modules:
  0.0 105.0 jit_solution(5105078273810037200)
XLA Ops:
  0.0 28.3 %exchange.1 = (bf16[32,512,128]{2,1,0:T(8,128)(2,1)S(1)}, bf16[16384,128]{1,0:T(8,128)(2,1)S(1)}, bf16[4,256,256]{2,1,0:T(8,128)(2,1)S(1)}, s32[32,128]{1,0:T(8,128)S(1)}, bf16[17,128,128]{2,1,0:T(8,128)(2,1)S(1)}) custom-call(bf16[512,1024]{1,0:T(8,128)(2,1)} %tok_hbm.1, bf16[1024,256]{1,0:T(8,128)(2,1)} %wq_hbm.1, bf16[1024,256]{1,0:T(8,128)(2,1)} %wk_hbm.1, ...), custom_call_target="tpu_custom_call" | custom-call | tf_op jit(solution)/shard_map/exchange/pallas_call | solution.py:284
  28.3 42.7 %attend.1.att_ref = bf16[4,256,128]{2,1,0:T(8,128)(2,1)S(1)} custom-call(s32[32,128]{1,0:T(8,128)S(1)} %get-tuple-element.10.lists, bf16[16384,128]{1,0:T(8,128)(2,1)S(1)} %bitcast.3, bf16[16384,128]{1,0:T(8,128)(2,1)S(1)} %get-tuple-element.12.ones_v, bf16[17,128,128]{2,1,0:T(8,128)(2,1)S(1)} %get-tuple-element.13.qz), custom_call_target="tpu_custom_call" | custom-call | tf_op jit(solution)/shard_map/attend/pallas_call | solution.py:391
  71.0 32.9 %give_back.1.att_ref = bf16[16,256,128]{2,1,0:T(8,128)(2,1)S(1)} custom-call(bf16[4,256,128]{2,1,0:T(8,128)(2,1)S(1)} %attend.1.att_ref), custom_call_target="tpu_custom_call" | custom-call | tf_op jit(solution)/shard_map/give_back/pallas_call | solution.py:495
  103.8 1.2 %mix.1 = bf16[512,256]{1,0:T(8,128)(2,1)} custom-call(bf16[16,256,128]{2,1,0:T(8,128)(2,1)S(1)} %give_back.1.att_ref, bf16[1024,256]{1,0:T(8,128)(2,1)S(1)} %bitcast.4), custom_call_target="tpu_custom_call" | custom-call | tf_op jit(solution)/shard_map/mix/pallas_call | solution.py:517

commit v4 on v3

--- a/solution.py
+++ b/solution.py
@@ -304,7 +304,7 @@
     )(*operands)
 
 
-UNROLL = 8
+UNROLL = 7
 EXP2_SCALE = (HEAD_DIM ** -0.5) * 1.4426950408889634
 SMALLEST, LARGEST = 1e-20, 1e30
 NT = (((1,), (1,)), ((), ()))
@@ -438,10 +438,21 @@
         copy.start()
         sent.append(copy)
 
-    for d in range(4):
+    def send_near(d):
+        send(att_ref.at[(y + d) % NY], all_ref.at[me_global], send_sems.at[d], recv_sems.at[d], near[d])
+
+    def send_cross(d):
         send(att_ref.at[(y + d) % NY], all_ref.at[me_global], send_sems.at[4 + d], recv_sems.at[4 + d], cross[d])
+
     here = remote(att_ref.at[y], all_ref.at[me_global], send_sems.at[0], recv_sems.at[0], near[0])
     local = pltpu.make_async_copy(att_ref.at[y], all_ref.at[me_global], recv_sems.at[0])
+    send_cross(2)
+    send_cross(1)
+    send_cross(3)
+    send_near(2)
+    send_cross(0)
+    send_near(1)
+    send_near(3)
 
     @pl.when(stays)
     def _():
@@ -450,9 +461,6 @@
     @pl.when(jnp.logical_not(stays))
     def _():
         here.start()
-
-    for d in range(1, 4):
-        send(att_ref.at[(y + d) % NY], all_ref.at[me_global], send_sems.at[d], recv_sems.at[d], near[d])
 
     def of(source_hi, source_lo, d):
         return all_ref.at[(source_hi * 2 + source_lo) * 4 + (y + NY - d) % NY]

time: 105 us -> 98.2 us (0.935)
  the two profiles are of different devices: /device:TPU:97 before, /device:TPU:65 now
where the time goes in v4:
time: 98.2 us; the launch traced here: 98.1 us
  Pallas kernels  98.1 us (100%)
    pallas_call x1, Pallas kernels, attend(): pl.pallas_call(attend_kernel, out_shape=jax.ShapeDtypeStruct((4, ROWS //...  54.3 us
    pallas_call x1, Pallas kernels, exchange(): pl.pallas_call(exchange_kernel, out_shape=(jax.ShapeDtypeStruct((32, ROWS...  28.1 us
    pallas_call x1, Pallas kernels, give_back(): pl.pallas_call(return_kernel, out_shape=jax.ShapeDtypeStruct((16, ROWS //...  14.5 us

profile of v4, /device:TPU:65, one launch (start us, length us, event | category | flops | bytes accessed | tf_op | source)
XLA Modules:
  0.0 98.1 jit_solution(5330385557085636156)
XLA Ops:
  0.0 28.1 %exchange.1 = (bf16[32,512,128]{2,1,0:T(8,128)(2,1)S(1)}, bf16[16384,128]{1,0:T(8,128)(2,1)S(1)}, bf16[4,256,256]{2,1,0:T(8,128)(2,1)S(1)}, s32[32,128]{1,0:T(8,128)S(1)}, bf16[17,128,128]{2,1,0:T(8,128)(2,1)S(1)}) custom-call(bf16[512,1024]{1,0:T(8,128)(2,1)} %tok_hbm.1, bf16[1024,256]{1,0:T(8,128)(2,1)} %wq_hbm.1, bf16[1024,256]{1,0:T(8,128)(2,1)} %wk_hbm.1, ...), custom_call_target="tpu_custom_call" | custom-call | tf_op jit(solution)/shard_map/exchange/pallas_call | solution.py:284
  28.1 54.3 %attend.1.att_ref = bf16[4,256,128]{2,1,0:T(8,128)(2,1)S(1)} custom-call(s32[32,128]{1,0:T(8,128)S(1)} %get-tuple-element.10.lists, bf16[16384,128]{1,0:T(8,128)(2,1)S(1)} %bitcast.3, bf16[16384,128]{1,0:T(8,128)(2,1)S(1)} %get-tuple-element.12.ones_v, bf16[17,128,128]{2,1,0:T(8,128)(2,1)S(1)} %get-tuple-element.13.qz), custom_call_target="tpu_custom_call" | custom-call | tf_op jit(solution)/shard_map/attend/pallas_call | solution.py:391
  82.4 14.5 %give_back.1.att_ref = bf16[16,256,128]{2,1,0:T(8,128)(2,1)S(1)} custom-call(bf16[4,256,128]{2,1,0:T(8,128)(2,1)S(1)} %attend.1.att_ref), custom_call_target="tpu_custom_call" | custom-call | tf_op jit(solution)/shard_map/give_back/pallas_call | solution.py:503
  96.9 1.2 %mix.1 = bf16[512,256]{1,0:T(8,128)(2,1)} custom-call(bf16[16,256,128]{2,1,0:T(8,128)(2,1)S(1)} %give_back.1.att_ref, bf16[1024,256]{1,0:T(8,128)(2,1)S(1)} %bitcast.4), custom_call_target="tpu_custom_call" | custom-call | tf_op jit(solution)/shard_map/mix/pallas_call | solution.py:525

commit v5 on v4

--- a/solution.py
+++ b/solution.py
@@ -129,14 +129,6 @@
     kv_local = pltpu.make_async_copy(kv_ref.at[own], kv_all.at[me_ctx], a_recv.at[0])
     q_local = pltpu.make_async_copy(q_ref.at[own], q_all.at[y], q_recv.at[0])
 
-    @pl.when(stays)
-    def _():
-        kv_local.start()
-
-    @pl.when(jnp.logical_not(stays))
-    def _():
-        kv_here.start()
-
     def send_kv(d):
         send(kv_ref.at[(y + d) % NY], kv_all.at[me_ctx], a_send.at[d], a_recv.at[d], a_to[d])
 
@@ -163,19 +155,30 @@
         send(above, above, c_send.at[8 + d], c_recv.at[8 + d], twin)
 
     order = (1, 3, 2)
+    onward = [(z_send.at[0], z_recv.at[0], up), (z_send.at[4], z_recv.at[4], down), (c_send.at[0], c_recv.at[0], twin)]
+
+    @pl.when(stays)
+    def _():
+        for send_sem, recv_sem, device in onward:
+            remote(kv_ref.at[own], kv_all.at[me_ctx], send_sem, recv_sem, device).start()
+        kv_local.start()
+
+    @pl.when(jnp.logical_not(stays))
+    def _():
+        kv_here.start()
+
     send_kv(1)
     send_kv(3)
     send_kv(2)
 
-    @pl.when(stays)
-    def _():
-        kv_local.wait()
-
     @pl.when(jnp.logical_not(stays))
     def _():
         kv_here.wait_recv()
-
-    pass_on(0)
+        for send_sem, recv_sem, device in onward:
+            remote(chunk(0, 0), chunk(0, 0), send_sem, recv_sem, device).start()
+
+    for send_sem, recv_sem, device in onward:
+        sent.append(remote(chunk(0, 0), chunk(0, 0), send_sem, recv_sem, device))
     loads[3].wait()
     query = jnp.dot(tok, wq_ref[...], preferred_element_type=F32).astype(BF16)
     for j in range(4):
@@ -227,6 +230,7 @@
     @pl.when(stays)
     def _():
         q_local.wait()
+        kv_local.wait()
 
     @pl.when(jnp.logical_not(stays))
     def _():
@@ -465,7 +469,7 @@
     def of(source_hi, source_lo, d):
         return all_ref.at[(source_hi * 2 + source_lo) * 4 + (y + NY - d) % NY]
 
-    for d in (0, 1, 3, 2):
+    def near_in(d):
         got = of(x_hi, core, d)
         if d == 0:
             @pl.when(stays)
@@ -478,10 +482,20 @@
         else:
             remote(got, got, send_sems.at[d], recv_sems.at[d], near[d]).wait_recv()
         send(got, got, c_send.at[d], c_recv.at[d], twin)
-    for d in (0, 1, 3, 2):
+
+    def cross_in(d):
         got = of(1 - x_hi, core, d)
         remote(got, got, send_sems.at[4 + d], recv_sems.at[4 + d], cross[d]).wait_recv()
         send(got, got, c_send.at[4 + d], c_recv.at[4 + d], twin)
+
+    near_in(0)
+    cross_in(0)
+    cross_in(1)
+    cross_in(3)
+    near_in(1)
+    near_in(3)
+    near_in(2)
+    cross_in(2)
     for d in (0, 1, 3, 2):
         got = of(x_hi, 1 - core, d)
         remote(got, got, c_send.at[d], c_recv.at[d], twin).wait_recv()

time: 98.2 us -> 109 us (1.11)
  the two profiles are of different devices: /device:TPU:65 before, /device:TPU:1 now
where the time goes in v5:
time: 109 us; the launch traced here: 108 us
  Pallas kernels  108 us (99%)
    pallas_call x1, Pallas kernels, attend(): pl.pallas_call(attend_kernel, out_shape=jax.ShapeDtypeStruct((4, ROWS //...  58.3 us
    pallas_call x1, Pallas kernels, exchange(): pl.pallas_call(exchange_kernel, out_shape=(jax.ShapeDtypeStruct((32, ROWS...  31.7 us
    pallas_call x1, Pallas kernels, give_back(): pl.pallas_call(return_kernel, out_shape=jax.ShapeDtypeStruct((16, ROWS //...  17.2 us

profile of v5, /device:TPU:1, one launch (start us, length us, event | category | flops | bytes accessed | tf_op | source)
XLA Modules:
  0.0 108.4 jit_solution(11210215935303994589)
XLA Ops:
  0.0 31.7 %exchange.1 = (bf16[32,512,128]{2,1,0:T(8,128)(2,1)S(1)}, bf16[16384,128]{1,0:T(8,128)(2,1)S(1)}, bf16[4,256,256]{2,1,0:T(8,128)(2,1)S(1)}, s32[32,128]{1,0:T(8,128)S(1)}, bf16[17,128,128]{2,1,0:T(8,128)(2,1)S(1)}) custom-call(bf16[512,1024]{1,0:T(8,128)(2,1)} %tok_hbm.1, bf16[1024,256]{1,0:T(8,128)(2,1)} %wq_hbm.1, bf16[1024,256]{1,0:T(8,128)(2,1)} %wk_hbm.1, ...), custom_call_target="tpu_custom_call" | custom-call | tf_op jit(solution)/shard_map/exchange/pallas_call | solution.py:288
  31.7 58.3 %attend.1.att_ref = bf16[4,256,128]{2,1,0:T(8,128)(2,1)S(1)} custom-call(s32[32,128]{1,0:T(8,128)S(1)} %get-tuple-element.10.lists, bf16[16384,128]{1,0:T(8,128)(2,1)S(1)} %bitcast.3, bf16[16384,128]{1,0:T(8,128)(2,1)S(1)} %get-tuple-element.12.ones_v, bf16[17,128,128]{2,1,0:T(8,128)(2,1)S(1)} %get-tuple-element.13.qz), custom_call_target="tpu_custom_call" | custom-call | tf_op jit(solution)/shard_map/attend/pallas_call | solution.py:395
  90.0 17.2 %give_back.1.att_ref = bf16[16,256,128]{2,1,0:T(8,128)(2,1)S(1)} custom-call(bf16[4,256,128]{2,1,0:T(8,128)(2,1)S(1)} %attend.1.att_ref), custom_call_target="tpu_custom_call" | custom-call | tf_op jit(solution)/shard_map/give_back/pallas_call | solution.py:517
  107.2 1.2 %mix.1 = bf16[512,256]{1,0:T(8,128)(2,1)} custom-call(bf16[16,256,128]{2,1,0:T(8,128)(2,1)S(1)} %give_back.1.att_ref, bf16[1024,256]{1,0:T(8,128)(2,1)S(1)} %bitcast.4), custom_call_target="tpu_custom_call" | custom-call | tf_op jit(solution)/shard_map/mix/pallas_call | solution.py:539

commit v6 on v5

--- a/solution.py
+++ b/solution.py
@@ -218,14 +218,18 @@
         got = kv_all.at[ctx_of((y + NY - d) % NY, (z + NZ + dz) % NZ, 1 - core)]
         arrived(got, c_send.at[place_of + d], c_recv.at[place_of + d], twin)
 
-    left = lax.broadcasted_iota(jnp.int32, (ROWS, 128), 1) < HEAD_DIM
-
     def lay_out(d, dz, sides=(0, 1)):
         for side in sides:
             ctx = ctx_of((y + NY - d) % NY, (z + NZ + dz) % NZ, side)
-            rows = pl.ds(pl.multiple_of(ctx * ROWS, ROWS), ROWS)
-            got = kv_all[ctx]
-            ones_v[rows, :] = jnp.where(left, jnp.ones_like(got), got)
+            for b in range(ROWS // BLOCK):
+                got = kv_all[ctx, b * BLOCK : (b + 1) * BLOCK, :].astype(F32)
+                ones_v[ctx * 4 + b, 16:80, :] = jnp.transpose(got)[HEAD_DIM:, :].astype(BF16)
+
+    def ones_of(block, _):
+        ones_v[block, 0:16, :] = jnp.ones((16, 128), BF16)
+        return 0
+
+    lax.fori_loop(0, NB, ones_of, 0)
 
     @pl.when(stays)
     def _():
@@ -246,22 +250,21 @@
             q = jnp.concatenate([q[:, HEAD_DIM:], q[:, :HEAD_DIM]], axis=1)
         qz[i] = jnp.where(narrow, q, jnp.zeros_like(q))
     qz[16] = jnp.zeros((BLOCK, 128), BF16)
+    from_near(3)
+    from_near(2)
     for d in (0, 1, 3, 2):
         twin_arrived(d, 0, 0)
         lay_out(d, 0)
-    from_near(3)
-    from_near(2)
     for d in (0, 1, 3, 2):
         twin_arrived(d, -1, 4)
         twin_arrived(d, 1, 8)
         lay_out(d, -1)
         lay_out(d, 1)
-    for d in (0, 1, 3, 2):
         far = chunk(d, 2)
         arrived(far, z_send.at[8 + d], z_recv.at[8 + d], up)
         send(far, far, c_send.at[12 + d], c_recv.at[12 + d], twin)
+    for d in (0, 1, 3, 2):
         lay_out(d, 2, (core,))
-    for d in (0, 1, 3, 2):
         twin_arrived(d, 2, 12)
         lay_out(d, 2, (1 - core,))
 
@@ -289,7 +292,7 @@
         exchange_kernel,
         out_shape=(
             jax.ShapeDtypeStruct((32, ROWS, 128), BF16),
-            jax.ShapeDtypeStruct((32 * ROWS, 128), BF16),
+            jax.ShapeDtypeStruct((NB, 80, BLOCK), BF16),
             jax.ShapeDtypeStruct((4, 256, 256), BF16),
             jax.ShapeDtypeStruct((32, NB), jnp.int32),
             jax.ShapeDtypeStruct((17, BLOCK, 128), BF16),
@@ -317,11 +320,14 @@
 def attend_kernel(lists, kv_ref, ones_v, qz, out_ref, acc, sbuf, scores):
     zero = jnp.zeros((BLOCK, 128), F32)
     for i in range(17):
-        acc[i] = zero
-    second = lax.broadcasted_iota(jnp.int32, (1, 2 * BLOCK), 1) >= BLOCK
+        acc[i] = jnp.zeros((80, BLOCK), F32)
+    second = lax.broadcasted_iota(jnp.int32, (2 * BLOCK, 1), 0) >= BLOCK
+
+    def block_at(i, k):
+        return lists[i, jnp.minimum(k, NB - 1)]
 
     def rows_at(i, k):
-        return pl.ds(pl.multiple_of(lists[i, jnp.minimum(k, NB - 1)] * BLOCK, BLOCK), BLOCK)
+        return pl.ds(pl.multiple_of(block_at(i, k) * BLOCK, BLOCK), BLOCK)
 
     def advance(i, k):
         done = k + 2 >= lists[17, i]
@@ -330,16 +336,16 @@
     def score(slot, i, k):
         for u in range(UNROLL):
             keys = jnp.concatenate([kv_ref[rows_at(i, k), :], kv_ref[rows_at(i, k + 1), :]], axis=0)
-            sbuf[slot, u] = lax.dot_general(qz[i], keys, NT, preferred_element_type=F32)
+            bias = jnp.where(k + 1 < lists[17, i], 0.0, LIST_PAD).astype(F32)
+            s = lax.dot_general(keys, qz[i], NT, preferred_element_type=F32)
+            sbuf[slot, u] = jnp.exp2(s * EXP2_SCALE + jnp.where(second, bias, 0.0)).astype(BF16)
             i, k = advance(i, k)
         return i, k
 
     def weigh(slot, i, k):
         for u in range(UNROLL):
-            bias = jnp.where(k + 1 < lists[17, i], 0.0, LIST_PAD).astype(F32)
-            vals = jnp.concatenate([ones_v[rows_at(i, k), :], ones_v[rows_at(i, k + 1), :]], axis=0)
-            p = jnp.exp2(sbuf[slot, u] * EXP2_SCALE + jnp.where(second, bias, 0.0)).astype(BF16)
-            acc[i] += jnp.dot(p, vals, preferred_element_type=F32)
+            vals = jnp.concatenate([ones_v[block_at(i, k)], ones_v[block_at(i, k + 1)]], axis=1)
+            acc[i] += jnp.dot(vals, sbuf[slot, u], preferred_element_type=F32)
             i, k = advance(i, k)
 
     start = jnp.int32(0)
@@ -355,13 +361,13 @@
 
     lax.fori_loop(0, (lists[17, 32] + 2 * UNROLL - 1) // (2 * UNROLL), step, (start, start, i1, k1))
 
-    fine = jnp.full((BLOCK, HEAD_DIM), 1.0, F32)
+    fine = jnp.full((1, BLOCK), 1.0, F32)
     for i in range(16):
         y, rows, cols = query_place(i)
-        denom = acc[i][:, :HEAD_DIM]
+        denom = acc[i][0:1, :]
         within = jnp.logical_and(denom >= SMALLEST, denom <= LARGEST)
         fine = jnp.where(within, fine, 0.0)
-        out_ref[y, rows, cols] = (acc[i][:, HEAD_DIM:] / denom).astype(BF16)
+        out_ref[y, rows, cols] = jnp.transpose(acc[i][16:80, :] / denom).astype(BF16)
 
     @pl.when(jnp.min(fine) < 0.5)
     def _():
@@ -401,8 +407,8 @@
             in_specs=[whole] * 3,
             out_specs=whole,
             scratch_shapes=[
-                vmem((17, BLOCK, 128), F32),
-                vmem((2, UNROLL, BLOCK, 2 * BLOCK), F32),
+                vmem((17, 80, BLOCK), F32),
+                vmem((2, UNROLL, 2 * BLOCK, BLOCK), BF16),
                 vmem((NB, BLOCK, BLOCK), F32),
             ],
         ),

time: 109 us -> 101 us (0.927)
  Pallas kernels: 108 us -> 100 us
    pallas_call x1, Pallas kernels: 58.3 us -> 51.2 us  [attend(): pl.pallas_call(attend_kernel, out_shape=jax.ShapeDtypeStruct((4, ROWS //...]
where the time goes in v6:
time: 101 us; the launch traced here: 100 us
  Pallas kernels  100 us (99%)
    pallas_call x1, Pallas kernels, attend(): pl.pallas_call(attend_kernel, out_shape=jax.ShapeDtypeStruct((4, ROWS //...  51.2 us
    pallas_call x1, Pallas kernels, exchange(): pl.pallas_call(exchange_kernel, out_shape=(jax.ShapeDtypeStruct((32, ROWS...  31.8 us
    pallas_call x1, Pallas kernels, give_back(): pl.pallas_call(return_kernel, out_shape=jax.ShapeDtypeStruct((16, ROWS //...  16.3 us

profile of v6, /device:TPU:1, one launch (start us, length us, event | category | flops | bytes accessed | tf_op | source)
XLA Modules:
  0.0 100.4 jit_solution(13756091232067320621)
XLA Ops:
  0.0 31.8 %exchange.1 = (bf16[32,512,128]{2,1,0:T(8,128)(2,1)S(1)}, bf16[128,80,128]{2,1,0:T(8,128)(2,1)S(1)}, bf16[4,256,256]{2,1,0:T(8,128)(2,1)S(1)}, s32[32,128]{1,0:T(8,128)S(1)}, bf16[17,128,128]{2,1,0:T(8,128)(2,1)S(1)}) custom-call(bf16[512,1024]{1,0:T(8,128)(2,1)} %tok_hbm.1, bf16[1024,256]{1,0:T(8,128)(2,1)} %wq_hbm.1, bf16[1024,256]{1,0:T(8,128)(2,1)} %wk_hbm.1, ...), custom_call_target="tpu_custom_call" | custom-call | tf_op jit(solution)/shard_map/exchange/pallas_call | solution.py:291
  31.8 51.2 %attend.1.att_ref = bf16[4,256,128]{2,1,0:T(8,128)(2,1)S(1)} custom-call(s32[32,128]{1,0:T(8,128)S(1)} %get-tuple-element.10.lists, bf16[16384,128]{1,0:T(8,128)(2,1)S(1)} %bitcast.3, bf16[128,80,128]{2,1,0:T(8,128)(2,1)S(1)} %get-tuple-element.12.ones_v, bf16[17,128,128]{2,1,0:T(8,128)(2,1)S(1)} %get-tuple-element.13.qz), custom_call_target="tpu_custom_call" | custom-call | tf_op jit(solution)/shard_map/attend/pallas_call | solution.py:401
  82.9 16.3 %give_back.1.att_ref = bf16[16,256,128]{2,1,0:T(8,128)(2,1)S(1)} custom-call(bf16[4,256,128]{2,1,0:T(8,128)(2,1)S(1)} %attend.1.att_ref), custom_call_target="tpu_custom_call" | custom-call | tf_op jit(solution)/shard_map/give_back/pallas_call | solution.py:523
  99.3 1.2 %mix.1 = bf16[512,256]{1,0:T(8,128)(2,1)} custom-call(bf16[16,256,128]{2,1,0:T(8,128)(2,1)S(1)} %give_back.1.att_ref, bf16[1024,256]{1,0:T(8,128)(2,1)S(1)} %bitcast.4), custom_call_target="tpu_custom_call" | custom-call | tf_op jit(solution)/shard_map/mix/pallas_call | solution.py:545
